TPU v7x, 512 devices: a whole 4x4x16 slice. The times are simulated.
512 devices in a mesh: row: 64 (over y_lo, z, core), col: 8 (over x, y_hi).
Axes of the slice: x: 4, y: 4 (y_hi: 2, y_lo: 2; y = y_hi * 2 + y_lo), z: 16, core: 2. Of those that a mesh axis runs over, the one named last changes fastest.
Arguments:
- mantissas: bfloat16 [512, 6144], P('row', 'col'), may hold values from -4 to 4
- block_exponents: int32 [512, 48], P('row', 'col'), may hold values from -2 to 1
- input_weight: bfloat16 [6144, 24576], P('col', 'row'), may hold values from -0.078125 to 0.078125
- input_noise: bfloat16 [6144, 24576], P('col', 'row'), may hold values from -0.0546875 to 0.0546875
- output_weight: bfloat16 [24576, 6144], P('row', 'col'), may hold values from -0.0390625 to 0.0390625
- output_noise: bfloat16 [24576, 6144], P('row', 'col'), may hold values from -0.02734375 to 0.02734375
- preactivation: bfloat16 [512, 24576], P(None, 'row'), may hold values from -6 to 6
- adc_mask: int32 [512, 192], P(None, 'row'), may hold values 0 or 1
- teacher: bfloat16 [512, 6144], P('row', 'col'), may hold values from -6 to 6
Outputs:
- input_grad: bfloat16 [512, 6144], P('row', 'col')
- first_grad: bfloat16 [6144, 24576], P('col', 'row')
- second_grad: bfloat16 [24576, 6144], P('row', 'col')
All inputs are finite; a program needn't handle non-finite values. No bound on the sum of `adc_mask` on one device may be relied on, other than what follows from the above.
Results may differ from a plain program's by a relative error of at most 0.022.
Values may be sent and summed in bfloat16 or wider, within the bound.
No kernel may reach another device: no remote copies, remote signals or barrier semaphores. Data moves between devices by JAX's collectives and lax.ppermute only.
A program may use at most 64 MiB of HBM per device.

v0:
```python
import jax
import jax.numpy as jnp
from jax import lax
from jax.sharding import PartitionSpec as P

adc_range = 1.5


def activation(hidden, mask):
    width = hidden.shape[1] // mask.shape[1]
    gelu = jax.nn.gelu(hidden, approximate=True)
    tiles = jnp.repeat(mask, width, axis=1)
    return jnp.where(tiles > 0, adc_range * jnp.tanh(gelu / adc_range), gelu)


def local(
    mantissas,
    block_exponents,
    input_weight,
    input_noise,
    output_weight,
    output_noise,
    preactivation,
    adc_mask,
    teacher,
):
    block_width = mantissas.shape[1] // block_exponents.shape[1]
    scales = jnp.repeat(jnp.exp2(block_exponents.astype(jnp.float32)), block_width, axis=1)
    features = (mantissas.astype(jnp.float32) * scales).astype(jnp.bfloat16)
    noisy_in = (input_weight.astype(jnp.float32) + input_noise.astype(jnp.float32)).astype(
        jnp.bfloat16
    )
    noisy_out = (output_weight.astype(jnp.float32) + output_noise.astype(jnp.float32)).astype(
        jnp.bfloat16
    )
    hidden = preactivation.astype(jnp.float32)
    total_rows = hidden.shape[0]
    inverse_root = total_rows ** (-0.5)
    values, pullback = jax.vjp(lambda v: activation(v, adc_mask), hidden)
    activated = values.astype(jnp.bfloat16)
    student = lax.psum_scatter(
        jnp.dot(activated, noisy_out, preferred_element_type=jnp.float32),
        "row",
        scatter_dimension=0,
        tiled=True,
    )
    residual = (student - teacher.astype(jnp.float32)).astype(jnp.bfloat16)
    piece = lax.all_gather(residual, "row", axis=0, tiled=True)
    grad_sum = jnp.dot(activated.T, piece, preferred_element_type=jnp.float32)
    fresh = jnp.dot(piece, noisy_out.T, preferred_element_type=jnp.float32)
    second_grad = (grad_sum * inverse_root).astype(jnp.bfloat16)
    summed = lax.psum(fresh.astype(jnp.bfloat16), "col").astype(jnp.float32)
    hidden_grad = pullback(summed)[0].astype(jnp.bfloat16)
    input_grad = lax.psum_scatter(
        jnp.dot(hidden_grad, noisy_in.T, preferred_element_type=jnp.float32),
        "row",
        scatter_dimension=0,
        tiled=True,
    ).astype(jnp.bfloat16)
    first_sum = jnp.dot(
        lax.all_gather(features, "row", axis=0, tiled=True).T,
        hidden_grad,
        preferred_element_type=jnp.float32,
    )
    first_grad = (first_sum * inverse_root).astype(jnp.bfloat16)
    return (input_grad, first_grad, second_grad)


def solution(mesh):
    placed = (
        P("row", "col"),
        P("row", "col"),
        P("col", "row"),
        P("col", "row"),
        P("row", "col"),
        P("row", "col"),
        P(None, "row"),
        P(None, "row"),
        P("row", "col"),
    )
    return jax.shard_map(
        local,
        mesh=mesh,
        in_specs=placed,
        out_specs=(P("row", "col"), P("col", "row"), P("row", "col")),
        check_vma=False,
    )
```

profile of v0, /device:TPU:1, one launch (start us, length us, event | category | flops | bytes accessed | tf_op | source)
XLA Modules:
  0.0 634.4 jit_solution(6469358402561756034)
XLA Ops:
  7.2 0.0 reduce-scatter.3.cloned.1.call-start
  7.2 0.7 broadcast_compare_fusion
  7.9 0.1 broadcast_in_dim.10
  8.0 0.3 copy.15
  8.3 3.4 fusion.16
  11.7 0.0 reduce-scatter.3.cloned.1.call-update
  11.7 0.0 all-reduce.2.cloned.1.call-start
  11.8 229.1 %reduce-scatter.3.cloned.1.call-done = f32[8,768]{1,0:T(8,128)} async-done(((f32[512,768]{1,0:T(8,128)}), f32[8,768]{1,0:T(8,128)}) %reduce-scatter.3.cloned.1.call-update) | async-done | bytes 24592 | tf_op jit(solution)/shard_map/reduce_scatter | solution.py:41
  240.9 0.7 subtract_convert_fusion
  241.7 65.6 %all_gather.6 = bf16[512,768]{1,0:T(8,128)(2,1)S(1)} all-gather(bf16[8,768]{1,0:T(8,128)(2,1)S(1)} %subtract_convert_fusion), channel_id=1, replica_groups=mesh['row'=64,'col'=8] {'row'}, dimensions={0}, use_global_device_ids=true | all-gather | bytes 798720 | tf_op jit(solution)/shard_map/all_gather | solution.py:48
  307.3 1.3 convolution_convert_fusion
  308.6 0.0 all-reduce.2.cloned.1.call-update
  308.7 0.0 reduce-scatter.5.cloned.1.call-start
  308.7 87.1 %all-reduce.2.cloned.1.call-done = bf16[512,384]{1,0:T(8,128)(2,1)} async-done(((bf16[512,384]{1,0:T(8,128)(2,1)}), bf16[512,384]{1,0:T(8,128)(2,1)}) %all-reduce.2.cloned.1.call-update) | async-done | bytes 393232 | tf_op jit(solution)/shard_map/psum | solution.py:52
  395.8 3.7 fusion.15
  399.5 0.0 reduce-scatter.5.cloned.1.call-update
  399.6 0.7 copy-done.2
  400.2 0.1 copy.17
  400.3 0.1 fusion.17
  400.4 70.9 %all_gather.7 = bf16[512,768]{1,0:T(8,128)(2,1)S(1)} all-gather(bf16[8,768]{1,0:T(8,128)(2,1)S(1)} %fusion.17), channel_id=1, replica_groups=mesh['row'=64,'col'=8] {'row'}, dimensions={0}, use_global_device_ids=true | all-gather | bytes 798720 | tf_op jit(solution)/shard_map/all_gather | solution.py:61
  471.3 1.6 fusion.1
  472.9 2.2 fusion
  475.1 151.4 %reduce-scatter.5.cloned.1.call-done = f32[8,768]{1,0:T(8,128)} async-done(((f32[512,768]{1,0:T(8,128)}), f32[8,768]{1,0:T(8,128)}) %reduce-scatter.5.cloned.1.call-update) | async-done | bytes 24592 | tf_op jit(solution)/shard_map/reduce_scatter | solution.py:54
  626.6 1.3 convert_element_type.70
  (18 shorter events, 0.0 us)
Async XLA Ops:
  7.2 233.8 %reduce-scatter.3.cloned.1.call-start = ((), (), s32[]{:S(2)}) async-start(), calls=%async_computation.2 | async-start | bytes 1597440 | tf_op jit(solution)/shard_map/reduce_scatter | solution.py:41
  11.7 229.2 %copy-start.1 = (bf16[8,768]{1,0:T(8,128)(2,1)S(1)}, bf16[8,768]{1,0:T(8,128)(2,1)}, u32[]{:S(2)}) copy-start(bf16[8,768]{1,0:T(8,128)(2,1)} %param.17) | copy-start | bytes 36868
  11.7 295.6 %copy-start.3 = (bf16[384,768]{1,0:T(8,128)(2,1)S(1)}, bf16[384,768]{1,0:T(8,128)(2,1)}, u32[]{:S(2)}) copy-start(bf16[384,768]{1,0:T(8,128)(2,1)} %param.14) | copy-start | bytes 1769476
  11.7 295.6 %copy-start.4 = (bf16[384,768]{1,0:T(8,128)(2,1)S(1)}, bf16[384,768]{1,0:T(8,128)(2,1)}, u32[]{:S(2)}) copy-start(bf16[384,768]{1,0:T(8,128)(2,1)} %param.13) | copy-start | bytes 1769476
  11.7 384.0 %all-reduce.2.cloned.1.call-start = ((), (), s32[]{:S(2)}) async-start(), calls=%async_computation.3 | async-start | bytes 786432 | tf_op jit(solution)/shard_map/psum | solution.py:52
  307.3 88.5 %copy-start.5 = (bf16[768,384]{1,0:T(8,128)(2,1)S(1)}, bf16[768,384]{1,0:T(8,128)(2,1)}, u32[]{:S(2)}) copy-start(bf16[768,384]{1,0:T(8,128)(2,1)} %param.12) | copy-start | bytes 1769476
  307.3 88.5 %copy-start.6 = (bf16[768,384]{1,0:T(8,128)(2,1)S(1)}, bf16[768,384]{1,0:T(8,128)(2,1)}, u32[]{:S(2)}) copy-start(bf16[768,384]{1,0:T(8,128)(2,1)} %param.11) | copy-start | bytes 1769476
  308.7 317.9 %reduce-scatter.5.cloned.1.call-start = ((), (), s32[]{:S(2)}) async-start(), calls=%async_computation.4 | async-start | bytes 1597440 | tf_op jit(solution)/shard_map/reduce_scatter | solution.py:54
  399.5 0.7 copy-start.2
  399.5 0.8 copy-start
  399.5 71.8 %copy-start.7 = (bf16[512,384]{1,0:T(8,128)(2,1)S(1)}, bf16[512,384]{1,0:T(8,128)(2,1)}, u32[]{:S(2)}) copy-start(bf16[512,384]{1,0:T(8,128)(2,1)} %param.15) | copy-start | bytes 1179652
  471.3 1.6 copy-start.8
Sparse Core Ops, SparseCore 0:
  11.9 229.0 reduce-scatter.2
  308.8 86.9 all-reduce.1
  399.7 226.8 reduce-scatter.4
where the time goes:
time: 638 us; the launch traced here: 634 us
  waiting for transfers between devices  468 us (73%)
  blocking collectives  137 us (21%)
  between operations  13.8 us (2%)
  matrix products  12.3 us (2%)
    reduce_scatter x1, waiting for transfers between devices, local(): lax.psum_scatter(jnp.dot(activated, noisy_out, preferred_element_type=jnp...  229 us
    reduce_scatter x1, waiting for transfers between devices, local(): lax.psum_scatter(jnp.dot(hidden_grad, noisy_in.T, preferred_element_type=...  151 us
    psum x1, waiting for transfers between devices, local(): summed = lax.psum(fresh.astype(jnp.bfloat16), 'col').astype(jnp.float32)  87.1 us
    all_gather x1, blocking collectives, local(): lax.all_gather(features, 'row', axis=0, tiled=True)  70.9 us
    all_gather x1, blocking collectives, local(): piece = lax.all_gather(residual, 'row', axis=0, tiled=True)  65.6 us
  transfers between devices with their start and end apart: 3, of which 3 were waited for; matrix products, arithmetic and copies ran while one was open for 1% of the time, Pallas kernels for 0%

commit v1 on v0

v1 whole, which is shorter than its diff:
```python
import jax
import jax.numpy as jnp
from jax import lax
from jax.sharding import PartitionSpec as P

adc_range = 1.5
bf16 = jnp.bfloat16
f32 = jnp.float32


def activation(hidden, mask):
    width = hidden.shape[1] // mask.shape[1]
    gelu = jax.nn.gelu(hidden, approximate=True)
    tiles = jnp.repeat(mask, width, axis=1)
    return jnp.where(tiles > 0, adc_range * jnp.tanh(gelu / adc_range), gelu)


def dot(a, b):
    return jnp.dot(a, b, preferred_element_type=f32)


def dot_t(a, b):
    return lax.dot_general(a, b, (((1,), (1,)), ((), ())), preferred_element_type=f32)


def t_dot(a, b):
    return lax.dot_general(a, b, (((0,), (0,)), ((), ())), preferred_element_type=f32)


def program(rows, cols):
    chips = rows // 2
    same_core = [[chip * 2 + core for chip in range(chips)] for core in range(2)]
    same_chip = [[chip * 2, chip * 2 + 1] for chip in range(chips)]
    swap = [(i, i ^ 1) for i in range(rows)]

    def by_core(a):
        total = a.shape[0]
        return a.reshape(chips, 2, total // rows, -1).swapaxes(0, 1).reshape(total, -1)

    def scatter_sum(left, right):
        core = lax.axis_index("row") % 2
        half = left.shape[0] // 2
        halves = left.reshape(2, half, -1)
        theirs = dot(lax.dynamic_index_in_dim(halves, 1 - core, 0, False), right)
        got = lax.ppermute(theirs.astype(bf16), "row", swap)
        ours = dot(lax.dynamic_index_in_dim(halves, core, 0, False), right)
        both = (ours + got.astype(f32)).astype(bf16).reshape(chips, half // chips, -1)
        parts = lax.all_to_all(both, "row", 0, 0, axis_index_groups=same_core, tiled=True)
        return jnp.sum(parts.astype(f32), axis=0)

    def local(
        mantissas,
        block_exponents,
        input_weight,
        input_noise,
        output_weight,
        output_noise,
        preactivation,
        adc_mask,
        teacher,
    ):
        block_width = mantissas.shape[1] // block_exponents.shape[1]
        scales = jnp.repeat(jnp.exp2(block_exponents.astype(f32)), block_width, axis=1)
        halved = lax.all_gather(mantissas.astype(f32) * (scales * 0.5), "row", axis=0, tiled=True)
        features = by_core((halved * 2.0).astype(bf16))
        noisy_in = (input_weight.astype(f32) + input_noise.astype(f32)).astype(bf16)
        noisy_out = (output_weight.astype(f32) + output_noise.astype(f32)).astype(bf16)
        hidden = by_core(preactivation)
        mask = by_core(adc_mask)
        tokens = hidden.shape[0]
        inverse_root = tokens ** (-0.5)
        activated = activation(hidden.astype(f32), mask).astype(bf16)

        student = scatter_sum(activated, noisy_out)
        residual = (student - teacher.astype(f32)).astype(bf16)
        piece = lax.all_to_all(
            jnp.broadcast_to(residual, (chips,) + residual.shape),
            "row",
            0,
            0,
            axis_index_groups=same_core,
            tiled=True,
        ).reshape(tokens // 2, -1)
        piece = lax.all_gather(piece, "row", axis=0, tiled=True, axis_index_groups=same_chip)

        fresh = dot_t(piece, noisy_out).astype(bf16).reshape(cols, tokens // cols, -1)
        second_grad = (t_dot(activated, piece) * inverse_root).astype(bf16)
        parts = lax.all_to_all(fresh, "col", 0, 0, tiled=True)
        summed = jnp.sum(parts.astype(f32), axis=0)
        share = tokens // cols
        start = lax.axis_index("col") * share
        own = lax.dynamic_slice_in_dim(hidden, start, share, 0).astype(f32)
        own_mask = lax.dynamic_slice_in_dim(mask, start, share, 0)
        pullback = jax.vjp(lambda v: activation(v, own_mask), own)[1]
        own_grad = pullback(summed)[0].astype(bf16)
        hidden_grad = lax.all_to_all(
            jnp.broadcast_to(own_grad, (cols,) + own_grad.shape), "col", 0, 0, tiled=True
        ).reshape(tokens, -1)
        input_grad = scatter_sum(hidden_grad, noisy_in.T).astype(bf16)
        first_grad = (t_dot(features, hidden_grad) * inverse_root).astype(bf16)
        return (input_grad, first_grad, second_grad)

    return local


def solution(mesh):
    placed = (
        P("row", "col"),
        P("row", "col"),
        P("col", "row"),
        P("col", "row"),
        P("row", "col"),
        P("row", "col"),
        P(None, "row"),
        P(None, "row"),
        P("row", "col"),
    )
    return jax.shard_map(
        program(mesh.shape["row"], mesh.shape["col"]),
        mesh=mesh,
        in_specs=placed,
        out_specs=(P("row", "col"), P("col", "row"), P("row", "col")),
        check_vma=False,
    )
```

time: 638 us -> 208 us (0.33)
  waiting for transfers between devices: 468 us -> 96.3 us
  blocking collectives: 137 us -> 53.3 us
  starting transfers between devices: 0.12 us -> 28.3 us
    reduce_scatter x2 -> x0, waiting for transfers between devices: 381 us -> none  [the longest x1 229 us: local(): lax.psum_scatter(jnp.dot(activated, noisy_out, preferred_element_type=jnp...]
    all_gather x2 -> x1, blocking collectives: 137 us -> 5.01 us  [local(): lax.all_gather(piece, 'row', axis=0, tiled=True, axis_index_groups=same_c...]
    psum x1 -> x0, waiting for transfers between devices: 87.1 us -> none  [local(): summed = lax.psum(fresh.astype(jnp.bfloat16), 'col').astype(jnp.float32)]
    all_gather x0 -> x1, waiting for transfers between devices: none -> 60.6 us  [local(): lax.all_gather(mantissas.astype(f32) * (scales * 0.5), 'row', axis=0, til...]
    all_to_all x0 -> x2, blocking collectives: none -> 48.3 us  [the longest x1 36.3 us: scatter_sum(): lax.all_to_all(both, 'row', 0, 0, axis_index_groups=same_core, tiled=True)]
    all_to_all x0 -> x3, waiting for transfers between devices: none -> 33 us  [the longest x1 24.1 us: local(): lax.all_to_all(jnp.broadcast_to(residual, (chips,) + residual.shape), 'ro...]
    all_to_all x0 -> x3, starting transfers between devices: none -> 15.2 us  [the longest x1 6.36 us: local(): parts = lax.all_to_all(fresh, 'col', 0, 0, tiled=True)]
    ppermute x0 -> x2, starting transfers between devices: none -> 13.1 us  [scatter_sum(): got = lax.ppermute(theirs.astype(bf16), 'row', swap)]
  transfers between devices with their start and end apart: 3 -> 6, of which waited for: 3 -> 5; matrix products, arithmetic and copies ran while one was open for 1% -> 4% of each run, Pallas kernels for 0% -> 0%
where the time goes in v1:
time: 208 us
  waiting for transfers between devices  96.3 us (46%)
  blocking collectives  53.3 us (26%)
  starting transfers between devices  28.3 us (14%)
  between operations  14.3 us (7%)
  matrix products  6.68 us (3%)
  local copies, waits for them, and re-layouts  4.88 us (2%)
  other arithmetic  3.67 us (2%)
    all_gather x1, waiting for transfers between devices, local(): lax.all_gather(mantissas.astype(f32) * (scales * 0.5), 'row', axis=0, til...  60.6 us
    all_to_all x1, blocking collectives, scatter_sum(): lax.all_to_all(both, 'row', 0, 0, axis_index_groups=same_core, tiled=True)  36.3 us
    all_to_all x1, waiting for transfers between devices, local(): lax.all_to_all(jnp.broadcast_to(residual, (chips,) + residual.shape), 'ro...  24.1 us
    ppermute x2, starting transfers between devices, scatter_sum(): got = lax.ppermute(theirs.astype(bf16), 'row', swap)  13.1 us
    all_to_all x1, blocking collectives, local(): lax.all_to_all(jnp.broadcast_to(own_grad, (cols,) + own_grad.shape), 'col...  12 us
    all_to_all x1, waiting for transfers between devices, local(): parts = lax.all_to_all(fresh, 'col', 0, 0, tiled=True)  8.88 us
    all_to_all x1, starting transfers between devices, local(): parts = lax.all_to_all(fresh, 'col', 0, 0, tiled=True)  6.36 us
    all_gather x1, blocking collectives, local(): lax.all_gather(piece, 'row', axis=0, tiled=True, axis_index_groups=same_c...  5.01 us
  transfers between devices with their start and end apart: 6, of which 5 were waited for; matrix products, arithmetic and copies ran while one was open for 4% of the time, Pallas kernels for 0%

profile of v1, /device:TPU:1, one launch (start us, length us, event | category | flops | bytes accessed | tf_op | source)
XLA Modules:
  0.0 207.5 jit_solution(10203142928762953723)
XLA Ops:
  7.2 1.0 reshape.55
  8.6 1.6 broadcast_in_dim.21.clone
  10.5 0.4 select_convert_fusion.1
  11.4 8.8 %collective-permute-start = (bf16[256,768]{1,0:T(8,128)(2,1)S(1)}, bf16[256,768]{1,0:T(8,128)(2,1)S(1)}, u32[]{:S(2)}, u32[]{:S(2)}) collective-permute-start(bf16[256,768]{1,0:T(8,128)(2,1)S(1)} %convolution_convert_fusion.2), channel_id=1, source_target_pairs={{0,8},{8,0},{16,24},{24,16},{32,40},{40,32},{48,56},{56,48},{64,72... | collective-permute-start | bytes 1179656 | tf_op jit(solution)/shard_map/ppermute | solution.py:45
  20.2 1.3 collective-permute-done
  21.9 36.3 %all_to_all.25 = bf16[32,8,768]{2,1,0:T(8,128)(2,1)S(1)} all-to-all(bf16[32,8,768]{2,1,0:T(8,128)(2,1)S(1)} %fusion.14), channel_id=1, replica_groups={{0,16,32,48,64,80,96,112,128,144,160,176,192,208,224,240,256,272,288,30..., dimensions={0} | all-to-all | bytes 786432 | tf_op jit(solution)/shard_map/all_to_all | solution.py:48
  58.3 0.8 broadcast_in_dim.22
  59.1 4.9 %all-to-all-start.1 = ((bf16[32,8,768]{2,1,0:T(8,128)(2,1)}), bf16[32,8,768]{2,1,0:T(8,128)(2,1)S(1)}, u32[]{:S(2)}, u32[]{:S(2)}) async-start(bf16[32,8,768]{2,1,0:T(8,128)(2,1)} %broadcast_in_dim.22), calls=%async_computation.1 | async-start | bytes 786432 | tf_op jit(solution)/shard_map/all_to_all | solution.py:76
  64.2 0.7 bitcast_multiply_fusion
  64.9 24.1 %all-to-all-done.1 = bf16[32,8,768]{2,1,0:T(8,128)(2,1)S(1)} async-done(((bf16[32,8,768]{2,1,0:T(8,128)(2,1)}), bf16[32,8,768]{2,1,0:T(8,128)(2,1)S(1)}, u32[]{:S(2)}, u32[]{:S(2)}) %all-to-all-start.1) | async-done | bytes 393248 | tf_op jit(solution)/shard_map/all_to_all | solution.py:76
  89.0 5.0 %all_gather.6 = bf16[512,768]{1,0:T(8,128)(2,1)S(1)} all-gather(bf16[256,768]{1,0:T(8,128)(2,1)S(1)} %bitcast.57), channel_id=1, replica_groups={{0,8},{16,24},{32,40},{48,56},{64,72},{80,88},{96,104},{112,120},{128,1..., dimensions={0}, use_global_device_ids=true | all-gather | bytes 1179648 | tf_op jit(solution)/shard_map/all_gather | solution.py:84
  94.0 1.3 convolution_convert_fusion
  95.4 6.4 %all-to-all-start.2 = ((bf16[8,64,384]{2,1,0:T(8,128)(2,1)}), bf16[8,64,384]{2,1,0:T(8,128)(2,1)S(1)}, u32[]{:S(2)}, u32[]{:S(2)}) async-start(bf16[8,64,384]{2,1,0:T(8,128)(2,1)} %bitcast.8), calls=%async_computation.2 | async-start | bytes 786432 | tf_op jit(solution)/shard_map/all_to_all | solution.py:88
  102.0 8.9 %all-to-all-done.2 = bf16[8,64,384]{2,1,0:T(8,128)(2,1)S(1)} async-done(((bf16[8,64,384]{2,1,0:T(8,128)(2,1)}), bf16[8,64,384]{2,1,0:T(8,128)(2,1)S(1)}, u32[]{:S(2)}, u32[]{:S(2)}) %all-to-all-start.2) | async-done | bytes 393248 | tf_op jit(solution)/shard_map/all_to_all | solution.py:88
  111.3 12.0 %all_to_all.26 = bf16[8,64,384]{2,1,0:T(8,128)(2,1)S(1)} all-to-all(bf16[8,64,384]{2,1,0:T(8,128)(2,1)S(1)} %broadcast_in_dim.23), channel_id=1, replica_groups=mesh['row'=64,'col'=8] {'col'}, dimensions={0} | all-to-all | bytes 786432 | tf_op jit(solution)/shard_map/all_to_all | solution.py:96
  123.7 4.3 %collective-permute-start.1 = (bf16[256,768]{1,0:T(8,128)(2,1)S(1)}, bf16[256,768]{1,0:T(8,128)(2,1)S(1)}, u32[]{:S(2)}, u32[]{:S(2)}) collective-permute-start(bf16[256,768]{1,0:T(8,128)(2,1)S(1)} %convolution_convert_fusion.1), channel_id=1, source_target_pairs={{0,8},{8,0},{16,24},{24,16},{32,40},{40,32},{48,56},{56,48},{64,72... | collective-permute-start | bytes 1179656 | tf_op jit(solution)/shard_map/ppermute | solution.py:45
  128.0 1.3 collective-permute-done.1
  129.4 1.1 fusion.15
  130.5 3.9 %all-to-all-start.4 = ((bf16[32,8,768]{2,1,0:T(8,128)(2,1)}), bf16[32,8,768]{2,1,0:T(8,128)(2,1)S(1)}, u32[]{:S(2)}, u32[]{:S(2)}) async-start(bf16[32,8,768]{2,1,0:T(8,128)(2,1)} %fusion.15), calls=%async_computation.4 | async-start | bytes 786432 | tf_op jit(solution)/shard_map/all_to_all | solution.py:48
  134.7 60.6 %all-gather.2.cloned.1.call-done = f32[512,768]{1,0:T(8,128)} async-done(((f32[8,768]{1,0:T(8,128)}), f32[512,768]{1,0:T(8,128)}) %all-gather.2.cloned.1.call-update) | async-done | bytes 1572880 | tf_op jit(solution)/shard_map/all_gather | solution.py:64
  195.4 1.5 multiply_convert_fusion
  197.0 1.6 fusion.1
  198.6 1.4 fusion
  200.0 0.7 reduce_sum.32
  (41 shorter events, 3.1 us)
Async XLA Ops:
  7.2 3.4 %copy-start.4 = (bf16[512,384]{1,0:T(8,128)(2,1)S(1)}, bf16[512,384]{1,0:T(8,128)(2,1)}, u32[]{:S(2)}) copy-start(bf16[512,384]{1,0:T(8,128)(2,1)} %param.15) | copy-start | bytes 1179652
  7.2 3.8 %copy-start = (bf16[384,768]{1,0:T(8,128)(2,1)S(1)}, bf16[384,768]{1,0:T(8,128)(2,1)}, u32[]{:S(2)}) copy-start(bf16[384,768]{1,0:T(8,128)(2,1)} %param.14) | copy-start | bytes 1769476
  7.2 3.8 %copy-start.1 = (bf16[384,768]{1,0:T(8,128)(2,1)S(1)}, bf16[384,768]{1,0:T(8,128)(2,1)}, u32[]{:S(2)}) copy-start(bf16[384,768]{1,0:T(8,128)(2,1)} %param.13) | copy-start | bytes 1769476
  11.4 10.1 %collective-permute-start = (bf16[256,768]{1,0:T(8,128)(2,1)S(1)}, bf16[256,768]{1,0:T(8,128)(2,1)S(1)}, u32[]{:S(2)}, u32[]{:S(2)}) collective-permute-start(bf16[256,768]{1,0:T(8,128)(2,1)S(1)} %convolution_convert_fusion.2), channel_id=1, source_target_pairs={{0,8},{8,0},{16,24},{24,16},{32,40},{40,32},{48,56},{56,48},{64,72... | collective-permute-start | bytes 1179656 | tf_op jit(solution)/shard_map/ppermute | solution.py:45
  20.2 38.1 %copy-start.5 = (bf16[8,768]{1,0:T(8,128)(2,1)S(1)}, bf16[8,768]{1,0:T(8,128)(2,1)}, u32[]{:S(2)}) copy-start(bf16[8,768]{1,0:T(8,128)(2,1)} %param.17) | copy-start | bytes 36868
  21.9 42.2 %copy-start.7 = (s32[8,6]{1,0:T(8,128)S(1)}, s32[8,6]{1,0:T(8,128)}, u32[]{:S(2)}) copy-start(s32[8,6]{1,0:T(8,128)} %param.10) | copy-start | bytes 580
  21.9 42.3 %copy-start.6 = (bf16[8,768]{1,0:T(8,128)(2,1)S(1)}, bf16[8,768]{1,0:T(8,128)(2,1)}, u32[]{:S(2)}) copy-start(bf16[8,768]{1,0:T(8,128)(2,1)} %param.9) | copy-start | bytes 36868
  59.1 29.9 %all-to-all-start.1 = ((bf16[32,8,768]{2,1,0:T(8,128)(2,1)}), bf16[32,8,768]{2,1,0:T(8,128)(2,1)S(1)}, u32[]{:S(2)}, u32[]{:S(2)}) async-start(bf16[32,8,768]{2,1,0:T(8,128)(2,1)} %broadcast_in_dim.22), calls=%async_computation.1 | async-start | bytes 786432 | tf_op jit(solution)/shard_map/all_to_all | solution.py:76
  64.1 131.3 %all-gather.2.cloned.1.call-start = ((), (), s32[]{:S(2)}) async-start(), calls=%async_computation.5 | async-start | bytes 1597440 | tf_op jit(solution)/shard_map/all_gather | solution.py:64
  95.4 15.5 %all-to-all-start.2 = ((bf16[8,64,384]{2,1,0:T(8,128)(2,1)}), bf16[8,64,384]{2,1,0:T(8,128)(2,1)S(1)}, u32[]{:S(2)}, u32[]{:S(2)}) async-start(bf16[8,64,384]{2,1,0:T(8,128)(2,1)} %bitcast.8), calls=%async_computation.2 | async-start | bytes 786432 | tf_op jit(solution)/shard_map/all_to_all | solution.py:88
  101.8 21.5 %copy-start.2 = (bf16[768,384]{1,0:T(8,128)(2,1)S(1)}, bf16[768,384]{1,0:T(8,128)(2,1)}, u32[]{:S(2)}) copy-start(bf16[768,384]{1,0:T(8,128)(2,1)} %param.12) | copy-start | bytes 1769476
  101.8 21.5 %copy-start.3 = (bf16[768,384]{1,0:T(8,128)(2,1)S(1)}, bf16[768,384]{1,0:T(8,128)(2,1)}, u32[]{:S(2)}) copy-start(bf16[768,384]{1,0:T(8,128)(2,1)} %param.11) | copy-start | bytes 1769476
  123.7 5.7 %collective-permute-start.1 = (bf16[256,768]{1,0:T(8,128)(2,1)S(1)}, bf16[256,768]{1,0:T(8,128)(2,1)S(1)}, u32[]{:S(2)}, u32[]{:S(2)}) collective-permute-start(bf16[256,768]{1,0:T(8,128)(2,1)S(1)} %convolution_convert_fusion.1), channel_id=1, source_target_pairs={{0,8},{8,0},{16,24},{24,16},{32,40},{40,32},{48,56},{56,48},{64,72... | collective-permute-start | bytes 1179656 | tf_op jit(solution)/shard_map/ppermute | solution.py:45
  130.5 69.5 %all-to-all-start.4 = ((bf16[32,8,768]{2,1,0:T(8,128)(2,1)}), bf16[32,8,768]{2,1,0:T(8,128)(2,1)S(1)}, u32[]{:S(2)}, u32[]{:S(2)}) async-start(bf16[32,8,768]{2,1,0:T(8,128)(2,1)} %fusion.15), calls=%async_computation.4 | async-start | bytes 786432 | tf_op jit(solution)/shard_map/all_to_all | solution.py:48
Sparse Core Ops, SparseCore 0:
  67.6 127.7 all-gather.1

commit v2 on v1

v2 whole, which is shorter than its diff:
```python
import jax
import jax.numpy as jnp
from jax import lax
from jax.sharding import PartitionSpec as P

adc_range = 1.5
bf16 = jnp.bfloat16
f32 = jnp.float32


def activation(hidden, mask):
    width = hidden.shape[1] // mask.shape[1]
    gelu = jax.nn.gelu(hidden, approximate=True)
    tiles = jnp.repeat(mask, width, axis=1)
    return jnp.where(tiles > 0, adc_range * jnp.tanh(gelu / adc_range), gelu)


def dot(a, b):
    return jnp.dot(a, b, preferred_element_type=f32)


def dot_t(a, b):
    return lax.dot_general(a, b, (((1,), (1,)), ((), ())), preferred_element_type=f32)


def t_dot(a, b):
    return lax.dot_general(a, b, (((0,), (0,)), ((), ())), preferred_element_type=f32)


def pick(a, i):
    return lax.dynamic_index_in_dim(a, i, 0, False)


def program(rows, cols):
    zs = rows // 4
    same_core = [[chip * 2 + core for chip in range(2 * zs)] for core in range(2)]
    along_z = [[(y * zs + z) * 2 + core for z in range(zs)] for y in range(2) for core in range(2)]
    swap_core = [(i, i ^ 1) for i in range(rows)]
    swap_y = [(i, (i + rows // 2) % rows) for i in range(rows)]

    def from_core(a):
        return lax.ppermute(a, "row", swap_core)

    def from_y(a):
        return lax.ppermute(a, "row", swap_y)

    def exchange(a, axis, groups=None):
        return lax.all_to_all(a, axis, 0, 0, axis_index_groups=groups, tiled=True)

    def spread(own, count, axis, groups=None):
        return exchange(jnp.broadcast_to(own, (count,) + own.shape), axis, groups)

    def add_up(parts):
        return jnp.sum(parts.astype(f32), axis=0)

    def of_four(own):
        pair = jnp.stack([own, from_y(own)])
        return jnp.concatenate([pair, from_core(pair)])

    def local(
        mantissas,
        block_exponents,
        input_weight,
        input_noise,
        output_weight,
        output_noise,
        preactivation,
        adc_mask,
        teacher,
    ):
        me = lax.axis_index("row")
        core, y = me % 2, me // (rows // 2)
        tokens, width = preactivation.shape
        model = mantissas.shape[1]
        quota = tokens // rows
        group = tokens // 4
        share = group // cols
        inverse_root = tokens ** (-0.5)

        block_width = model // block_exponents.shape[1]
        scales = jnp.repeat(jnp.exp2(block_exponents.astype(f32)), block_width, axis=1)
        features = (mantissas.astype(f32) * scales).astype(bf16)
        noisy_out = (output_weight.astype(f32) + output_noise.astype(f32)).astype(bf16)
        noisy_in = (input_weight.astype(f32) + input_noise.astype(f32)).astype(bf16)

        def by_group(a):
            return a.reshape(2, zs, 2, quota, -1).transpose(2, 0, 1, 3, 4)

        hidden = by_group(preactivation)
        mask = by_group(adc_mask)
        activated = activation(
            hidden.reshape(tokens, width).astype(f32), mask.reshape(tokens, -1)
        ).astype(bf16)

        pair = activated.reshape(2, 2 * group, width)
        theirs = from_core(dot(pick(pair, 1 - core), noisy_out).astype(bf16))
        both = dot(pick(pair, core), noisy_out) + theirs.astype(f32)
        both = both.astype(bf16).reshape(2 * zs, quota, model)
        student = add_up(exchange(both, "row", same_core))
        residual = (student - teacher.astype(f32)).astype(bf16)

        all_out = of_four(noisy_out).reshape(4 * width, model)
        all_in = of_four(noisy_in)
        all_in = jnp.concatenate([all_in[i] for i in range(4)], axis=1)
        first = lax.axis_index("col") * share
        own = lax.dynamic_slice_in_dim(hidden.reshape(4, group, width), first, share, 1)
        own_mask = lax.dynamic_slice_in_dim(mask.reshape(4, group, -1), first, share, 1)
        own_mask = own_mask.reshape(4 * share, -1)
        own = own.reshape(4 * share, width).astype(f32)
        slope = jax.vjp(lambda v: activation(v, own_mask), own)[1](jnp.ones_like(own))[0]
        slope = slope.reshape(2, 2, share, width).swapaxes(0, 1)
        slope = jnp.stack([pick(slope, y), from_y(pick(slope, 1 - y))], axis=1)
        slope = jnp.concatenate([pick(slope, core), from_core(pick(slope, 1 - core))])
        slope = slope.swapaxes(0, 1).reshape(share, 4 * width)

        sent = jnp.concatenate([residual, features])
        got = spread(sent, zs, "row", along_z)
        piece = got[:, :quota].reshape(group, model)
        fresh = dot_t(piece, all_out).astype(bf16).reshape(cols, share, 4 * width)
        own_grad = (add_up(exchange(fresh, "col")) * slope).astype(bf16)
        hidden_grad = spread(own_grad, cols, "col").reshape(group, 4 * width)

        partial = dot_t(hidden_grad, all_in).astype(bf16).reshape(zs, quota, model)
        input_grad = add_up(exchange(partial, "row", along_z)).astype(bf16)

        all_got = of_four(got)
        all_piece = all_got[:, :, :quota].reshape(tokens, model)
        all_features = all_got[:, :, quota:].reshape(tokens, model)
        near = pick(activated.reshape(2, 2, group, width), core)
        far = pick(activated.reshape(2, 2, group, width), 1 - core)
        all_activated = jnp.concatenate(
            [pick(near, y), pick(near, 1 - y), pick(far, y), pick(far, 1 - y)]
        )
        second_grad = (t_dot(all_activated, all_piece) * inverse_root).astype(bf16)

        blocks = [hidden_grad[:, i * width : (i + 1) * width] for i in range(4)]
        over = from_y(jnp.stack([blocks[1], blocks[3]]))
        other = from_core(jnp.stack([blocks[2], over[1]]))
        all_grad = jnp.concatenate([blocks[0], over[0], other[0], other[1]])
        first_grad = (t_dot(all_features, all_grad) * inverse_root).astype(bf16)
        return (input_grad, first_grad, second_grad)

    return local


def solution(mesh):
    placed = (
        P("row", "col"),
        P("row", "col"),
        P("col", "row"),
        P("col", "row"),
        P("row", "col"),
        P("row", "col"),
        P(None, "row"),
        P(None, "row"),
        P("row", "col"),
    )
    return jax.shard_map(
        program(mesh.shape["row"], mesh.shape["col"]),
        mesh=mesh,
        in_specs=placed,
        out_specs=(P("row", "col"), P("col", "row"), P("row", "col")),
        check_vma=False,
    )
```

time: 208 us -> 158 us (0.76)
  the two profiles are of different devices: /device:TPU:1 before, /device:TPU:56 now
where the time goes in v2:
time: 158 us; the launch traced here: 157 us
  starting transfers between devices  70.1 us (44%)
  waiting for transfers between devices  55.7 us (35%)
  local copies, waits for them, and re-layouts  11.1 us (7%)
  other arithmetic  9.78 us (6%)
  matrix products  8.68 us (5%)
    all_to_all x5, waiting for transfers between devices, exchange(): return lax.all_to_all(a, axis, 0, 0, axis_index_groups=groups, tiled=True)  47.1 us
    all_to_all x5, starting transfers between devices, exchange(): return lax.all_to_all(a, axis, 0, 0, axis_index_groups=groups, tiled=True)  43 us
    ppermute x5, starting transfers between devices, from_y(): return lax.ppermute(a, 'row', swap_y)  15.3 us
    ppermute x6, starting transfers between devices, from_core(): return lax.ppermute(a, 'row', swap_core)  11.8 us
    ppermute x5, waiting for transfers between devices, from_y(): return lax.ppermute(a, 'row', swap_y)  6.08 us
    dot_general x2, matrix products, dot_t(): lax.dot_general(a, b, (((1,), (1,)), ((), ())), preferred_element_type=f32)  4.46 us
  transfers between devices with their start and end apart: 16, of which 8 were waited for; matrix products, arithmetic and copies ran while one was open for 13% of the time, Pallas kernels for 0%

profile of v2, /device:TPU:56, one launch (start us, length us, event | category | flops | bytes accessed | tf_op | source)
XLA Modules:
  0.0 156.6 jit_solution(2768899922165829177)
XLA Ops:
  7.1 1.9 %collective-permute-start = (bf16[256,768]{1,0:T(8,128)(2,1)S(1)}, bf16[256,768]{1,0:T(8,128)(2,1)S(1)}, u32[]{:S(2)}, u32[]{:S(2)}) collective-permute-start(bf16[256,768]{1,0:T(8,128)(2,1)S(1)} %convolution_convert_fusion.1), channel_id=1, source_target_pairs={{0,8},{8,0},{16,24},{24,16},{32,40},{40,32},{48,56},{56,48},{64,72... | collective-permute-start | bytes 1179656 | tf_op jit(solution)/shard_map/ppermute | solution.py:42
  11.9 16.3 %all-to-all-start = ((bf16[32,8,768]{2,1,0:T(8,128)(2,1)}), bf16[32,8,768]{2,1,0:T(8,128)(2,1)S(1)}, u32[]{:S(2)}, u32[]{:S(2)}) async-start(bf16[32,8,768]{2,1,0:T(8,128)(2,1)} %fusion.30), calls=%async_computation | async-start | bytes 786432 | tf_op jit(solution)/shard_map/all_to_all | solution.py:48
  28.1 2.5 %collective-permute-start.1 = (bf16[384,768]{1,0:T(8,128)(2,1)S(1)}, bf16[384,768]{1,0:T(8,128)(2,1)S(1)}, u32[]{:S(2)}, u32[]{:S(2)}) collective-permute-start(bf16[384,768]{1,0:T(8,128)(2,1)S(1)} %add_convert_fusion.1), channel_id=1, source_target_pairs={{0,256},{8,264},{16,272},{24,280},{32,288},{40,296},{48,304},{56,3... | collective-permute-start | bytes 1769480 | tf_op jit(solution)/shard_map/ppermute | solution.py:45
  30.8 23.1 %all-to-all-done = bf16[32,8,768]{2,1,0:T(8,128)(2,1)S(1)} async-done(((bf16[32,8,768]{2,1,0:T(8,128)(2,1)}), bf16[32,8,768]{2,1,0:T(8,128)(2,1)S(1)}, u32[]{:S(2)}, u32[]{:S(2)}) %all-to-all-start) | async-done | bytes 393248 | tf_op jit(solution)/shard_map/all_to_all | solution.py:48
  54.8 4.4 %all-to-all-start.1 = ((bf16[16,16,768]{2,1,0:T(8,128)(2,1)}), bf16[16,16,768]{2,1,0:T(8,128)(2,1)S(1)}, u32[]{:S(2)}, u32[]{:S(2)}) async-start(bf16[16,16,768]{2,1,0:T(8,128)(2,1)} %broadcast_in_dim.23), calls=%async_computation.1 | async-start | bytes 786432 | tf_op jit(solution)/shard_map/all_to_all | solution.py:48
  59.3 1.9 %collective-permute-start.2 = (bf16[2,384,768]{2,1,0:T(8,128)(2,1)S(1)}, bf16[2,384,768]{2,1,0:T(8,128)(2,1)}, u32[]{:S(2)}, u32[]{:S(2)}) collective-permute-start(bf16[2,384,768]{2,1,0:T(8,128)(2,1)S(1)} %pad_maximum_fusion.2), channel_id=1, source_target_pairs={{0,8},{8,0},{16,24},{24,16},{32,40},{40,32},{48,56},{56,48},{64,72... | collective-permute-start | bytes 3538952 | tf_op jit(solution)/shard_map/ppermute | solution.py:42
  63.8 3.3 %collective-permute-start.3 = (f32[2,16,384]{2,1,0:T(8,128)S(1)}, f32[2,16,384]{2,1,0:T(8,128)S(1)}, u32[]{:S(2)}, u32[]{:S(2)}) collective-permute-start(f32[2,16,384]{2,1,0:T(8,128)S(1)} %get-tuple-element.23), channel_id=1, source_target_pairs={{0,256},{8,264},{16,272},{24,280},{32,288},{40,296},{48,304},{56,3... | collective-permute-start | bytes 147464 | tf_op jit(solution)/shard_map/ppermute | solution.py:45
  67.2 2.2 %add_convert_fusion = bf16[768,384]{1,0:T(8,128)(2,1)} fusion(bf16[768,384]{1,0:T(8,128)(2,1)} %param.12, bf16[768,384]{1,0:T(8,128)(2,1)} %param.11), kind=kLoop, calls=%fused_computation.20 | loop fusion | flops 1179648 | bytes 1769472 | tf_op jit(solution)/shard_map/convert_element_type | solution.py:84
  69.4 2.5 %collective-permute-start.5 = (bf16[768,384]{1,0:T(8,128)(2,1)}, bf16[768,384]{1,0:T(8,128)(2,1)}, u32[]{:S(2)}, u32[]{:S(2)}) collective-permute-start(bf16[768,384]{1,0:T(8,128)(2,1)} %add_convert_fusion), channel_id=1, source_target_pairs={{0,256},{8,264},{16,272},{24,280},{32,288},{40,296},{48,304},{56,3... | collective-permute-start | bytes 1769480 | tf_op jit(solution)/shard_map/ppermute | solution.py:45
  73.6 7.2 %all-to-all-done.1 = bf16[16,16,768]{2,1,0:T(8,128)(2,1)S(1)} async-done(((bf16[16,16,768]{2,1,0:T(8,128)(2,1)}), bf16[16,16,768]{2,1,0:T(8,128)(2,1)S(1)}, u32[]{:S(2)}, u32[]{:S(2)}) %all-to-all-start.1) | async-done | bytes 393248 | tf_op jit(solution)/shard_map/all_to_all | solution.py:48
  82.4 7.3 %all-to-all-start.2 = ((bf16[8,16,1536]{2,1,0:T(8,128)(2,1)}), bf16[8,16,1536]{2,1,0:T(8,128)(2,1)S(1)}, u32[]{:S(2)}, u32[]{:S(2)}) async-start(bf16[8,16,1536]{2,1,0:T(8,128)(2,1)} %bitcast.113), calls=%async_computation.2 | async-start | bytes 786432 | tf_op jit(solution)/shard_map/all_to_all | solution.py:48
  89.7 1.9 %collective-permute-start.4 = (f32[2,16,384]{2,1,0:T(8,128)S(1)}, f32[2,16,384]{2,1,0:T(8,128)S(1)}, u32[]{:S(2)}, u32[]{:S(2)}) collective-permute-start(f32[2,16,384]{2,1,0:T(8,128)S(1)} %get-tuple-element.22), channel_id=1, source_target_pairs={{0,8},{8,0},{16,24},{24,16},{32,40},{40,32},{48,56},{56,48},{64,72... | collective-permute-start | bytes 147464 | tf_op jit(solution)/shard_map/ppermute | solution.py:42
  92.9 2.4 %pad_maximum_fusion.3 = bf16[2,768,384]{2,1,0:T(8,128)(2,1)} fusion(bf16[1,768,384]{2,1,0:T(8,128)(2,1)} %bitcast.28, bf16[1,768,384]{2,1,0:T(8,128)(2,1)} %bitcast.27), kind=kLoop, calls=%fused_computation.19 | loop fusion | flops 589824 | bytes 2359296 | tf_op jit(solution)/shard_map/stack | solution.py:57
  95.3 2.2 %collective-permute-start.6 = (bf16[2,768,384]{2,1,0:T(8,128)(2,1)}, bf16[2,768,384]{2,1,0:T(8,128)(2,1)S(1)}, u32[]{:S(2)}, u32[]{:S(2)}) collective-permute-start(bf16[2,768,384]{2,1,0:T(8,128)(2,1)} %pad_maximum_fusion.3), channel_id=1, source_target_pairs={{0,8},{8,0},{16,24},{24,16},{32,40},{40,32},{48,56},{56,48},{64,72... | collective-permute-start | bytes 3538952 | tf_op jit(solution)/shard_map/ppermute | solution.py:42
  98.3 7.2 %all-to-all-start.3 = ((bf16[8,16,1536]{2,1,0:T(8,128)(2,1)}), bf16[8,16,1536]{2,1,0:T(8,128)(2,1)S(1)}, u32[]{:S(2)}, u32[]{:S(2)}) async-start(bf16[8,16,1536]{2,1,0:T(8,128)(2,1)} %broadcast_in_dim.27), calls=%async_computation.3 | async-start | bytes 786432 | tf_op jit(solution)/shard_map/all_to_all | solution.py:48
  106.1 3.5 %collective-permute-start.7 = (bf16[16,16,768]{2,1,0:T(8,128)(2,1)S(1)}, bf16[16,16,768]{2,1,0:T(8,128)(2,1)S(1)}, u32[]{:S(2)}, u32[]{:S(2)}) collective-permute-start(bf16[16,16,768]{2,1,0:T(8,128)(2,1)S(1)} %all-to-all-done.1), channel_id=1, source_target_pairs={{0,256},{8,264},{16,272},{24,280},{32,288},{40,296},{48,304},{56,3... | collective-permute-start | bytes 1179656 | tf_op jit(solution)/shard_map/ppermute | solution.py:45
  109.6 4.0 %all-to-all-done.3 = bf16[8,16,1536]{2,1,0:T(8,128)(2,1)S(1)} async-done(((bf16[8,16,1536]{2,1,0:T(8,128)(2,1)}), bf16[8,16,1536]{2,1,0:T(8,128)(2,1)S(1)}, u32[]{:S(2)}, u32[]{:S(2)}) %all-to-all-start.3) | async-done | bytes 393248 | tf_op jit(solution)/shard_map/all_to_all | solution.py:48
  114.3 3.5 %collective-permute-start.9 = (bf16[2,128,384]{2,1,0:T(8,128)(2,1)S(1)}, bf16[2,128,384]{2,1,0:T(8,128)(2,1)S(1)}, u32[]{:S(2)}, u32[]{:S(2)}) collective-permute-start(bf16[2,128,384]{2,1,0:T(8,128)(2,1)S(1)} %pad_maximum_fusion.5), channel_id=1, source_target_pairs={{0,256},{8,264},{16,272},{24,280},{32,288},{40,296},{48,304},{56,3... | collective-permute-start | bytes 589832 | tf_op jit(solution)/shard_map/ppermute | solution.py:45
  117.9 4.0 %collective-permute-done.7 = bf16[16,16,768]{2,1,0:T(8,128)(2,1)S(1)} collective-permute-done((bf16[16,16,768]{2,1,0:T(8,128)(2,1)S(1)}, bf16[16,16,768]{2,1,0:T(8,128)(2,1)S(1)}, u32[]{:S(2)}, u32[]{:S(2)}) %collective-permute-start.7) | collective-permute-done | bytes 393248 | tf_op jit(solution)/shard_map/ppermute | solution.py:45
  122.0 1.9 %collective-permute-start.8 = (bf16[2,16,16,768]{3,2,1,0:T(8,128)(2,1)S(1)}, bf16[2,16,16,768]{3,2,1,0:T(8,128)(2,1)S(1)}, u32[]{:S(2)}, u32[]{:S(2)}) collective-permute-start(bf16[2,16,16,768]{3,2,1,0:T(8,128)(2,1)S(1)} %pad_maximum_fusion.4), channel_id=1, source_target_pairs={{0,8},{8,0},{16,24},{24,16},{32,40},{40,32},{48,56},{56,48},{64,72... | collective-permute-start | bytes 2359304 | tf_op jit(solution)/shard_map/ppermute | solution.py:42
  123.9 2.1 %collective-permute-done.9 = bf16[2,128,384]{2,1,0:T(8,128)(2,1)S(1)} collective-permute-done((bf16[2,128,384]{2,1,0:T(8,128)(2,1)S(1)}, bf16[2,128,384]{2,1,0:T(8,128)(2,1)S(1)}, u32[]{:S(2)}, u32[]{:S(2)}) %collective-permute-start.9) | collective-permute-done | bytes 196640 | tf_op jit(solution)/shard_map/ppermute | solution.py:45
  128.6 2.8 %fusion.13 = bf16[16,8,768]{2,1,0:T(8,128)(2,1)} fusion(bf16[128,1536]{1,0:T(8,128)(2,1)S(1)} %bitcast.112, bf16[768,384]{1,0:T(8,128)(2,1)S(1)} %get-tuple-element.8, bf16[768,384]{1,0:T(8,128)(2,1)S(1)} %get-tuple-element.7, bf16[768,384]{1,0:T(8,128)(2,1)} %collective-permute-done.5, bf16[768,384]{1,0:T(8,128)(2,1)} %add_convert_fusion), kind=kOutput, calls=%fused_computation.23 | convolution fusion | flops 311525376 | bytes 2949120 | tf_op jit(solution)/shard_map/dot_general | solution.py:23
  131.4 7.8 %all-to-all-start.4 = ((bf16[16,8,768]{2,1,0:T(8,128)(2,1)}), bf16[16,8,768]{2,1,0:T(8,128)(2,1)S(1)}, u32[]{:S(2)}, u32[]{:S(2)}) async-start(bf16[16,8,768]{2,1,0:T(8,128)(2,1)} %fusion.13), calls=%async_computation.4 | async-start | bytes 393216 | tf_op jit(solution)/shard_map/all_to_all | solution.py:48
  143.2 12.7 %all-to-all-done.4 = bf16[16,8,768]{2,1,0:T(8,128)(2,1)S(1)} async-done(((bf16[16,8,768]{2,1,0:T(8,128)(2,1)}), bf16[16,8,768]{2,1,0:T(8,128)(2,1)S(1)}, u32[]{:S(2)}, u32[]{:S(2)}) %all-to-all-start.4) | async-done | bytes 196640 | tf_op jit(solution)/shard_map/all_to_all | solution.py:48
  (89 shorter events, 26.6 us)
Async XLA Ops:
  0.6 4.4 %copy-start.5 = (bf16[384,768]{1,0:T(8,128)(2,1)S(1)}, bf16[384,768]{1,0:T(8,128)(2,1)}, u32[]{:S(2)}) copy-start(bf16[384,768]{1,0:T(8,128)(2,1)} %param.14) | copy-start | bytes 1769476
  6.7 23.9 %copy-start.10 = (s32[8,6]{1,0:T(8,128)S(1)}, s32[8,6]{1,0:T(8,128)}, u32[]{:S(2)}) copy-start(s32[8,6]{1,0:T(8,128)} %param.10) | copy-start | bytes 580
  6.7 24.0 %copy-start.8 = (bf16[8,768]{1,0:T(8,128)(2,1)S(1)}, bf16[8,768]{1,0:T(8,128)(2,1)}, u32[]{:S(2)}) copy-start(bf16[8,768]{1,0:T(8,128)(2,1)} %param.9) | copy-start | bytes 36868
  7.1 46.9 %copy-start.9 = (bf16[8,768]{1,0:T(8,128)(2,1)S(1)}, bf16[8,768]{1,0:T(8,128)(2,1)}, u32[]{:S(2)}) copy-start(bf16[8,768]{1,0:T(8,128)(2,1)} %param.17) | copy-start | bytes 36868
  7.1 3.6 %collective-permute-start = (bf16[256,768]{1,0:T(8,128)(2,1)S(1)}, bf16[256,768]{1,0:T(8,128)(2,1)S(1)}, u32[]{:S(2)}, u32[]{:S(2)}) collective-permute-start(bf16[256,768]{1,0:T(8,128)(2,1)S(1)} %convolution_convert_fusion.1), channel_id=1, source_target_pairs={{0,8},{8,0},{16,24},{24,16},{32,40},{40,32},{48,56},{56,48},{64,72... | collective-permute-start | bytes 1179656 | tf_op jit(solution)/shard_map/ppermute | solution.py:42
  11.9 42.0 %all-to-all-start = ((bf16[32,8,768]{2,1,0:T(8,128)(2,1)}), bf16[32,8,768]{2,1,0:T(8,128)(2,1)S(1)}, u32[]{:S(2)}, u32[]{:S(2)}) async-start(bf16[32,8,768]{2,1,0:T(8,128)(2,1)} %fusion.30), calls=%async_computation | async-start | bytes 786432 | tf_op jit(solution)/shard_map/all_to_all | solution.py:48
  28.1 31.1 %collective-permute-start.1 = (bf16[384,768]{1,0:T(8,128)(2,1)S(1)}, bf16[384,768]{1,0:T(8,128)(2,1)S(1)}, u32[]{:S(2)}, u32[]{:S(2)}) collective-permute-start(bf16[384,768]{1,0:T(8,128)(2,1)S(1)} %add_convert_fusion.1), channel_id=1, source_target_pairs={{0,256},{8,264},{16,272},{24,280},{32,288},{40,296},{48,304},{56,3... | collective-permute-start | bytes 1769480 | tf_op jit(solution)/shard_map/ppermute | solution.py:45
  54.8 6.5 %copy-start = (bf16[512,384]{1,0:T(8,128)(2,1)S(1)}, bf16[512,384]{1,0:T(8,128)(2,1)}, u32[]{:S(2)}) copy-start(bf16[512,384]{1,0:T(8,128)(2,1)} %param.15) | copy-start | bytes 1179652
  54.8 26.0 %all-to-all-start.1 = ((bf16[16,16,768]{2,1,0:T(8,128)(2,1)}), bf16[16,16,768]{2,1,0:T(8,128)(2,1)S(1)}, u32[]{:S(2)}, u32[]{:S(2)}) async-start(bf16[16,16,768]{2,1,0:T(8,128)(2,1)} %broadcast_in_dim.23), calls=%async_computation.1 | async-start | bytes 786432 | tf_op jit(solution)/shard_map/all_to_all | solution.py:48
  59.2 2.9 %copy-start.2 = (bf16[384,768]{1,0:T(8,128)(2,1)}, bf16[384,768]{1,0:T(8,128)(2,1)S(1)}, u32[]{:S(2)}) copy-start(bf16[384,768]{1,0:T(8,128)(2,1)S(1)} %collective-permute-done.1) | copy-start | bytes 1769476
  59.3 12.6 %collective-permute-start.2 = (bf16[2,384,768]{2,1,0:T(8,128)(2,1)S(1)}, bf16[2,384,768]{2,1,0:T(8,128)(2,1)}, u32[]{:S(2)}, u32[]{:S(2)}) collective-permute-start(bf16[2,384,768]{2,1,0:T(8,128)(2,1)S(1)} %pad_maximum_fusion.2), channel_id=1, source_target_pairs={{0,8},{8,0},{16,24},{24,16},{32,40},{40,32},{48,56},{56,48},{64,72... | collective-permute-start | bytes 3538952 | tf_op jit(solution)/shard_map/ppermute | solution.py:42
  63.8 25.9 %collective-permute-start.3 = (f32[2,16,384]{2,1,0:T(8,128)S(1)}, f32[2,16,384]{2,1,0:T(8,128)S(1)}, u32[]{:S(2)}, u32[]{:S(2)}) collective-permute-start(f32[2,16,384]{2,1,0:T(8,128)S(1)} %get-tuple-element.23), channel_id=1, source_target_pairs={{0,256},{8,264},{16,272},{24,280},{32,288},{40,296},{48,304},{56,3... | collective-permute-start | bytes 147464 | tf_op jit(solution)/shard_map/ppermute | solution.py:45
  69.4 23.5 %collective-permute-start.5 = (bf16[768,384]{1,0:T(8,128)(2,1)}, bf16[768,384]{1,0:T(8,128)(2,1)}, u32[]{:S(2)}, u32[]{:S(2)}) collective-permute-start(bf16[768,384]{1,0:T(8,128)(2,1)} %add_convert_fusion), channel_id=1, source_target_pairs={{0,256},{8,264},{16,272},{24,280},{32,288},{40,296},{48,304},{56,3... | collective-permute-start | bytes 1769480 | tf_op jit(solution)/shard_map/ppermute | solution.py:45
  80.8 10.8 %copy-start.4 = (pred[512,3,128]{2,1,0:T(4,128)(4,1)S(1)}, pred[512,3,128]{2,1,0:T(4,128)(4,1)}, u32[]{:S(2)}) copy-start(pred[512,3,128]{2,1,0:T(4,128)(4,1)} %copy-done.3) | copy-start | bytes 589828
  82.4 15.0 %all-to-all-start.2 = ((bf16[8,16,1536]{2,1,0:T(8,128)(2,1)}), bf16[8,16,1536]{2,1,0:T(8,128)(2,1)S(1)}, u32[]{:S(2)}, u32[]{:S(2)}) async-start(bf16[8,16,1536]{2,1,0:T(8,128)(2,1)} %bitcast.113), calls=%async_computation.2 | async-start | bytes 786432 | tf_op jit(solution)/shard_map/all_to_all | solution.py:48
  89.7 3.1 %collective-permute-start.4 = (f32[2,16,384]{2,1,0:T(8,128)S(1)}, f32[2,16,384]{2,1,0:T(8,128)S(1)}, u32[]{:S(2)}, u32[]{:S(2)}) collective-permute-start(f32[2,16,384]{2,1,0:T(8,128)S(1)} %get-tuple-element.22), channel_id=1, source_target_pairs={{0,8},{8,0},{16,24},{24,16},{32,40},{40,32},{48,56},{56,48},{64,72... | collective-permute-start | bytes 147464 | tf_op jit(solution)/shard_map/ppermute | solution.py:42
  95.3 10.3 %copy-start.1 = (bf16[512,384]{1,0:T(8,128)(2,1)S(1)}, bf16[512,384]{1,0:T(8,128)(2,1)}, u32[]{:S(2)}) copy-start(bf16[512,384]{1,0:T(8,128)(2,1)} %param.15) | copy-start | bytes 1179652
  95.3 22.5 %collective-permute-start.6 = (bf16[2,768,384]{2,1,0:T(8,128)(2,1)}, bf16[2,768,384]{2,1,0:T(8,128)(2,1)S(1)}, u32[]{:S(2)}, u32[]{:S(2)}) collective-permute-start(bf16[2,768,384]{2,1,0:T(8,128)(2,1)} %pad_maximum_fusion.3), channel_id=1, source_target_pairs={{0,8},{8,0},{16,24},{24,16},{32,40},{40,32},{48,56},{56,48},{64,72... | collective-permute-start | bytes 3538952 | tf_op jit(solution)/shard_map/ppermute | solution.py:42
  98.3 15.2 %all-to-all-start.3 = ((bf16[8,16,1536]{2,1,0:T(8,128)(2,1)}), bf16[8,16,1536]{2,1,0:T(8,128)(2,1)S(1)}, u32[]{:S(2)}, u32[]{:S(2)}) async-start(bf16[8,16,1536]{2,1,0:T(8,128)(2,1)} %broadcast_in_dim.27), calls=%async_computation.3 | async-start | bytes 786432 | tf_op jit(solution)/shard_map/all_to_all | solution.py:48
  106.1 15.9 %collective-permute-start.7 = (bf16[16,16,768]{2,1,0:T(8,128)(2,1)S(1)}, bf16[16,16,768]{2,1,0:T(8,128)(2,1)S(1)}, u32[]{:S(2)}, u32[]{:S(2)}) collective-permute-start(bf16[16,16,768]{2,1,0:T(8,128)(2,1)S(1)} %all-to-all-done.1), channel_id=1, source_target_pairs={{0,256},{8,264},{16,272},{24,280},{32,288},{40,296},{48,304},{56,3... | collective-permute-start | bytes 1179656 | tf_op jit(solution)/shard_map/ppermute | solution.py:45
  114.3 11.7 %collective-permute-start.9 = (bf16[2,128,384]{2,1,0:T(8,128)(2,1)S(1)}, bf16[2,128,384]{2,1,0:T(8,128)(2,1)S(1)}, u32[]{:S(2)}, u32[]{:S(2)}) collective-permute-start(bf16[2,128,384]{2,1,0:T(8,128)(2,1)S(1)} %pad_maximum_fusion.5), channel_id=1, source_target_pairs={{0,256},{8,264},{16,272},{24,280},{32,288},{40,296},{48,304},{56,3... | collective-permute-start | bytes 589832 | tf_op jit(solution)/shard_map/ppermute | solution.py:45
  122.0 17.3 %collective-permute-start.8 = (bf16[2,16,16,768]{3,2,1,0:T(8,128)(2,1)S(1)}, bf16[2,16,16,768]{3,2,1,0:T(8,128)(2,1)S(1)}, u32[]{:S(2)}, u32[]{:S(2)}) collective-permute-start(bf16[2,16,16,768]{3,2,1,0:T(8,128)(2,1)S(1)} %pad_maximum_fusion.4), channel_id=1, source_target_pairs={{0,8},{8,0},{16,24},{24,16},{32,40},{40,32},{48,56},{56,48},{64,72... | collective-permute-start | bytes 2359304 | tf_op jit(solution)/shard_map/ppermute | solution.py:42
  126.7 12.6 %collective-permute-start.10 = (bf16[2,128,384]{2,1,0:T(8,128)(2,1)S(1)}, bf16[2,128,384]{2,1,0:T(8,128)(2,1)S(1)}, u32[]{:S(2)}, u32[]{:S(2)}) collective-permute-start(bf16[2,128,384]{2,1,0:T(8,128)(2,1)S(1)} %pad_maximum_fusion.6), channel_id=1, source_target_pairs={{0,8},{8,0},{16,24},{24,16},{32,40},{40,32},{48,56},{56,48},{64,72... | collective-permute-start | bytes 589832 | tf_op jit(solution)/shard_map/ppermute | solution.py:42
  131.4 24.5 %all-to-all-start.4 = ((bf16[16,8,768]{2,1,0:T(8,128)(2,1)}), bf16[16,8,768]{2,1,0:T(8,128)(2,1)S(1)}, u32[]{:S(2)}, u32[]{:S(2)}) async-start(bf16[16,8,768]{2,1,0:T(8,128)(2,1)} %fusion.13), calls=%async_computation.4 | async-start | bytes 393216 | tf_op jit(solution)/shard_map/all_to_all | solution.py:48
  (3 other events, 4.5 us)

commit v3 on v2

v3 whole, which is shorter than its diff:
```python
import functools

import jax
import jax.numpy as jnp
from jax import lax
from jax.experimental import pallas as pl
from jax.experimental.pallas import tpu as pltpu
from jax.sharding import PartitionSpec as P

adc_range = 1.5
bf16 = jnp.bfloat16
f32 = jnp.float32


def activation(hidden, mask):
    width = hidden.shape[1] // mask.shape[1]
    gelu = jax.nn.gelu(hidden, approximate=True)
    tiles = jnp.repeat(mask, width, axis=1)
    return jnp.where(tiles > 0, adc_range * jnp.tanh(gelu / adc_range), gelu)


def dot(a, b):
    return jnp.dot(a, b, preferred_element_type=f32)


def dot_t(a, b):
    return lax.dot_general(a, b, (((1,), (1,)), ((), ())), preferred_element_type=f32)


def t_dot(a, b):
    return lax.dot_general(a, b, (((0,), (0,)), ((), ())), preferred_element_type=f32)


def pick(a, i):
    return lax.dynamic_index_in_dim(a, i, 0, False)


whole = pl.BlockSpec(memory_space=pltpu.VMEM)
scalar = pl.BlockSpec(memory_space=pltpu.SMEM)
anywhere = pl.BlockSpec(memory_space=pl.ANY)
params = pltpu.CompilerParams(vmem_limit_bytes=40 * 2**20)


def shape(*dims):
    return jax.ShapeDtypeStruct(dims, bf16)


def start_kernel(quota, core_ref, pre_ref, mask_ref, w_ref, n_ref, act_ref, out_ref, theirs_ref):
    out_ref[...] = (w_ref[...].astype(f32) + n_ref[...].astype(f32)).astype(bf16)
    tokens, width = pre_ref.shape
    tiles = mask_ref.shape[1]
    tile = width // tiles
    step = min(128, tokens)
    for first in range(0, tokens, step):
        for j in range(tiles):
            columns = slice(j * tile, (j + 1) * tile)
            hidden = pre_ref[first : first + step, columns].astype(f32)
            gelu = jax.nn.gelu(hidden, approximate=True)
            value = jnp.where(
                mask_ref[first : first + step, j : j + 1] > 0,
                adc_range * jnp.tanh(gelu / adc_range),
                gelu,
            )
            value = value.reshape(step // (2 * quota), 2, quota, tile)
            for c in range(2):
                part = value[:, c].reshape(step // 2, tile).astype(bf16)
                act_ref[c, first // 2 : (first + step) // 2, columns] = part
    theirs = dot(act_ref[1 - core_ref[0]], out_ref[...])
    theirs_ref[...] = theirs.astype(bf16)


def residual_kernel(parts_ref, teacher_ref, features_ref, *refs):
    out_ref = refs[-1]
    total = parts_ref[0].astype(f32)
    for i in range(1, parts_ref.shape[0]):
        total += parts_ref[i].astype(f32)
    residual = (total - teacher_ref[...].astype(f32)).astype(bf16)
    block = jnp.concatenate([residual.astype(f32), features_ref[...].astype(f32)]).astype(bf16)
    for i in range(out_ref.shape[0]):
        out_ref[i] = block


def rows_kernel(got_ref, rows_ref):
    count, twice, model = got_ref.shape
    got = got_ref[...].astype(f32)
    for i in range(2):
        half = got[:, i * twice // 2 : (i + 1) * twice // 2].reshape(count * twice // 2, model)
        rows_ref[:, i * model : (i + 1) * model] = half.astype(bf16)


def input_kernel(grad_ref, a_ref, b_ref, c_ref, d_ref, partial_ref, *refs):
    width = a_ref.shape[1]
    block = [grad_ref[:, i * width : (i + 1) * width] for i in range(4)]
    total = dot_t(block[0], a_ref[...])
    for one, ref in zip(block[1:], (b_ref, c_ref, d_ref)):
        total += dot_t(one, ref[...])
    partial_ref[...] = total.astype(bf16)
    for one, ref in zip(block[1:], refs):
        ref[...] = one


def pair_kernel(a_ref, b_ref, after_ref, pair_ref):
    pair_ref[0] = a_ref[...]
    pair_ref[1] = b_ref[...]


def grads_kernel(scale, at_ref, act_ref, grad_ref, near_ref, far_ref, y_ref, core_ref, both_ref, first_ref, second_ref):
    width, model = second_ref.shape
    c, y = at_ref[0], at_ref[1]
    act = [act_ref[c, y], act_ref[c, 1 - y], act_ref[1 - c, y], act_ref[1 - c, 1 - y]]
    rows = [(ref, i) for ref in (near_ref, far_ref) for i in range(2)]
    residual = [ref[i, :, :model] for ref, i in rows]
    features = [ref[i, :, model:] for ref, i in rows]
    grad = [grad_ref[:, :width]] + [ref[...] for ref in (y_ref, core_ref, both_ref)]
    second = t_dot(jnp.concatenate(act), jnp.concatenate(residual))
    second_ref[...] = (second * scale).astype(bf16)
    first = t_dot(jnp.concatenate(features), jnp.concatenate(grad))
    first_ref[...] = (first * scale).astype(bf16)


def program(rows, cols):
    zs = rows // 4
    same_core = [[chip * 2 + core for chip in range(2 * zs)] for core in range(2)]
    along_z = [[(y * zs + z) * 2 + core for z in range(zs)] for y in range(2) for core in range(2)]
    swap_core = [(i, i ^ 1) for i in range(rows)]
    swap_both = [(i, (i ^ 1) + (rows // 2 if i < rows // 2 else -(rows // 2))) for i in range(rows)]
    swap_y = [(i, (i + rows // 2) % rows) for i in range(rows)]

    def from_core(a):
        return lax.ppermute(a, "row", swap_core)

    def from_y(a):
        return lax.ppermute(a, "row", swap_y)

    def from_both(a):
        return lax.ppermute(a, "row", swap_both)

    def exchange(a, axis, groups=None):
        return lax.all_to_all(a, axis, 0, 0, axis_index_groups=groups, tiled=True)

    def spread(own, count, axis, groups=None):
        return exchange(jnp.broadcast_to(own, (count,) + own.shape), axis, groups)

    def add_up(parts):
        return jnp.sum(parts.astype(f32), axis=0)

    def of_four(own):
        pair = jnp.stack([own, from_y(own)])
        return jnp.concatenate([pair, from_core(pair)])

    def local(
        mantissas,
        block_exponents,
        input_weight,
        input_noise,
        output_weight,
        output_noise,
        preactivation,
        adc_mask,
        teacher,
    ):
        me = lax.axis_index("row")
        core, y = me % 2, me // (rows // 2)
        tokens, width = preactivation.shape
        model = mantissas.shape[1]
        quota = tokens // rows
        group = tokens // 4
        share = group // cols
        inverse_root = tokens ** (-0.5)

        block_width = model // block_exponents.shape[1]
        scales = jnp.repeat(jnp.exp2(block_exponents.astype(f32)), block_width, axis=1)
        features = (mantissas.astype(f32) * scales).astype(bf16)
        noisy_in = (input_weight.astype(f32) + input_noise.astype(f32)).astype(bf16)

        activated, noisy_out, theirs = pl.pallas_call(
            functools.partial(start_kernel, quota),
            out_shape=(shape(2, 2 * group, width), shape(width, model), shape(2 * group, model)),
            in_specs=[pl.BlockSpec(memory_space=pltpu.SMEM)] + [whole] * 4,
            out_specs=(whole,) * 3,
            compiler_params=params,
            cost_estimate=pl.CostEstimate(
                flops=tokens * width * model, bytes_accessed=3 * 2**20, transcendentals=2 * tokens * width
            ),
        )(core[None], preactivation, adc_mask, output_weight, output_noise)

        both = dot(pick(activated, core), noisy_out) + from_core(theirs).astype(f32)
        both = both.astype(bf16).reshape(2 * zs, quota, model)
        parts = exchange(both, "row", same_core)

        all_out = of_four(noisy_out).reshape(4 * width, model)
        all_in = of_four(noisy_in)
        place = lax.axis_index("col")
        own = pick(preactivation.reshape(2, cols, 2 * share, width).swapaxes(0, 1), place)
        own_mask = pick(adc_mask.reshape(2, cols, 2 * share, -1).swapaxes(0, 1), place)
        own_mask = own_mask.reshape(4 * share, -1)
        own = own.reshape(4 * share, width).astype(f32)
        slope = jax.vjp(lambda v: activation(v, own_mask), own)[1](jnp.ones_like(own))[0]
        slope = slope.reshape(2, share // quota, 2, quota, width).swapaxes(1, 2)
        slope = slope.reshape(2, 2, share, width)
        slope = jnp.stack([pick(slope, y), from_y(pick(slope, 1 - y))], axis=1)
        slope = jnp.concatenate([pick(slope, core), from_core(pick(slope, 1 - core))])
        slope = slope.swapaxes(0, 1).reshape(share, 4 * width)

        sent = pl.pallas_call(
            residual_kernel,
            out_shape=shape(zs, 2 * quota, model),
            in_specs=[whole] * 3 + [anywhere] * 2,
            out_specs=whole,
            compiler_params=params,
            cost_estimate=pl.CostEstimate(flops=2**18, bytes_accessed=2**20, transcendentals=0),
        )(parts, teacher, features, all_out, slope)
        got = exchange(sent, "row", along_z)
        piece = got[:, :quota].reshape(group, model)
        fresh = dot_t(piece, all_out).astype(bf16).reshape(cols, share, 4 * width)
        own_grad = (add_up(exchange(fresh, "col")) * slope).astype(bf16)
        hidden_grad = spread(own_grad, cols, "col").reshape(group, 4 * width)

        own_rows = pl.pallas_call(
            rows_kernel,
            out_shape=shape(group, 2 * model),
            in_specs=[whole],
            out_specs=whole,
            compiler_params=params,
            cost_estimate=pl.CostEstimate(flops=0, bytes_accessed=2**20, transcendentals=0),
        )(got)
        partial, for_y, for_core, for_both = pl.pallas_call(
            input_kernel,
            out_shape=(shape(group, model),) + (shape(group, width),) * 3,
            in_specs=[whole] * 5,
            out_specs=(whole,) * 4,
            compiler_params=params,
            cost_estimate=pl.CostEstimate(
                flops=8 * group * width * model, bytes_accessed=3 * 2**20, transcendentals=0
            ),
        )(hidden_grad, *[all_in[i] for i in range(4)])
        partial = partial.reshape(zs, quota, model)
        input_grad = add_up(exchange(partial, "row", along_z)).astype(bf16)

        near_rows = pl.pallas_call(
            pair_kernel,
            out_shape=shape(2, group, 2 * model),
            in_specs=[whole] * 2 + [anywhere],
            out_specs=whole,
            compiler_params=params,
            cost_estimate=pl.CostEstimate(flops=0, bytes_accessed=3 * 2**19, transcendentals=0),
        )(own_rows, from_y(own_rows), partial)
        first_grad, second_grad = pl.pallas_call(
            functools.partial(grads_kernel, inverse_root),
            out_shape=(shape(model, width), shape(width, model)),
            in_specs=[scalar] + [whole] * 7,
            out_specs=(whole,) * 2,
            compiler_params=params,
            cost_estimate=pl.CostEstimate(
                flops=4 * tokens * width * model, bytes_accessed=2**21, transcendentals=0
            ),
        )(
            jnp.stack([core, y]),
            activated.reshape(2, 2, group, width),
            hidden_grad,
            near_rows,
            from_core(near_rows),
            from_y(for_y),
            from_core(for_core),
            from_both(for_both),
        )
        return (input_grad, first_grad, second_grad)

    return local


def solution(mesh):
    placed = (
        P("row", "col"),
        P("row", "col"),
        P("col", "row"),
        P("col", "row"),
        P("row", "col"),
        P("row", "col"),
        P(None, "row"),
        P(None, "row"),
        P("row", "col"),
    )
    return jax.shard_map(
        program(mesh.shape["row"], mesh.shape["col"]),
        mesh=mesh,
        in_specs=placed,
        out_specs=(P("row", "col"), P("col", "row"), P("row", "col")),
        check_vma=False,
    )
```

time: 158 us -> 152 us (0.962)
  the two profiles are of different devices: /device:TPU:56 before, /device:TPU:32 now
where the time goes in v3:
time: 152 us; the launch traced here: 151 us
  starting transfers between devices  70.9 us (47%)
  waiting for transfers between devices  54.3 us (36%)
  local copies, waits for them, and re-layouts  9.18 us (6%)
  Pallas kernels  7.34 us (5%)
  other arithmetic  5.42 us (4%)
  matrix products  2.76 us (2%)
    all_to_all x5, starting transfers between devices, exchange(): return lax.all_to_all(a, axis, 0, 0, axis_index_groups=groups, tiled=True)  42 us
    all_to_all x5, waiting for transfers between devices, exchange(): return lax.all_to_all(a, axis, 0, 0, axis_index_groups=groups, tiled=True)  35.4 us
    ppermute x5, waiting for transfers between devices, from_y(): return lax.ppermute(a, 'row', swap_y)  16.3 us
    ppermute x5, starting transfers between devices, from_y(): return lax.ppermute(a, 'row', swap_y)  15.3 us
    ppermute x6, starting transfers between devices, from_core(): return lax.ppermute(a, 'row', swap_core)  11.6 us
    unnamed x30, local copies, waits for them, and re-layouts  5.39 us
  transfers between devices with their start and end apart: 17, of which 9 were waited for; matrix products, arithmetic and copies ran while one was open for 8% of the time, Pallas kernels for 2%

profile of v3, /device:TPU:32, one launch (start us, length us, event | category | flops | bytes accessed | tf_op | source)
XLA Modules:
  0.0 150.9 jit_solution(12219320472612253413)
XLA Ops:
  5.5 3.5 %collective-permute-start.1 = (bf16[384,768]{1,0:T(8,128)(2,1)S(1)}, bf16[384,768]{1,0:T(8,128)(2,1)S(1)}, u32[]{:S(2)}, u32[]{:S(2)}) collective-permute-start(bf16[384,768]{1,0:T(8,128)(2,1)S(1)} %get-tuple-element.13), channel_id=1, source_target_pairs={{0,256},{8,264},{16,272},{24,280},{32,288},{40,296},{48,304},{56,3... | collective-permute-start | bytes 1769480 | tf_op jit(solution)/shard_map/ppermute | solution.py:133
  9.0 1.9 %collective-permute-start = (bf16[256,768]{1,0:T(8,128)(2,1)S(1)}, bf16[256,768]{1,0:T(8,128)(2,1)S(1)}, u32[]{:S(2)}, u32[]{:S(2)}) collective-permute-start(bf16[256,768]{1,0:T(8,128)(2,1)S(1)} %get-tuple-element.14), channel_id=1, source_target_pairs={{0,8},{8,0},{16,24},{24,16},{32,40},{40,32},{48,56},{56,48},{64,72... | collective-permute-start | bytes 1179656 | tf_op jit(solution)/shard_map/ppermute | solution.py:130
  13.8 15.4 %all-to-all-start = ((bf16[32,8,768]{2,1,0:T(8,128)(2,1)}), bf16[32,8,768]{2,1,0:T(8,128)(2,1)S(1)}, u32[]{:S(2)}, u32[]{:S(2)}) async-start(bf16[32,8,768]{2,1,0:T(8,128)(2,1)} %fusion), calls=%async_computation | async-start | bytes 786432 | tf_op jit(solution)/shard_map/all_to_all | solution.py:139
  30.0 2.0 %collective-permute-start.2 = (bf16[2,384,768]{2,1,0:T(8,128)(2,1)S(1)}, bf16[2,384,768]{2,1,0:T(8,128)(2,1)}, u32[]{:S(2)}, u32[]{:S(2)}) collective-permute-start(bf16[2,384,768]{2,1,0:T(8,128)(2,1)S(1)} %pad_maximum_fusion.1), channel_id=1, source_target_pairs={{0,8},{8,0},{16,24},{24,16},{32,40},{40,32},{48,56},{56,48},{64,72... | collective-permute-start | bytes 3538952 | tf_op jit(solution)/shard_map/ppermute | solution.py:130
  33.6 3.4 %collective-permute-start.3 = (f32[2,16,384]{2,1,0:T(8,128)S(1)}, f32[2,16,384]{2,1,0:T(8,128)S(1)}, u32[]{:S(2)}, u32[]{:S(2)}) collective-permute-start(f32[2,16,384]{2,1,0:T(8,128)S(1)} %get-tuple-element.25), channel_id=1, source_target_pairs={{0,256},{8,264},{16,272},{24,280},{32,288},{40,296},{48,304},{56,3... | collective-permute-start | bytes 147464 | tf_op jit(solution)/shard_map/ppermute | solution.py:133
  37.1 2.6 %collective-permute-done.3 = f32[2,16,384]{2,1,0:T(8,128)S(1)} collective-permute-done((f32[2,16,384]{2,1,0:T(8,128)S(1)}, f32[2,16,384]{2,1,0:T(8,128)S(1)}, u32[]{:S(2)}, u32[]{:S(2)}) %collective-permute-start.3) | collective-permute-done | bytes 49184 | tf_op jit(solution)/shard_map/ppermute | solution.py:133
  39.7 1.9 %collective-permute-start.4 = (f32[2,16,384]{2,0,1:T(2,128)S(1)}, f32[2,16,384]{2,0,1:T(2,128)S(1)}, u32[]{:S(2)}, u32[]{:S(2)}) collective-permute-start(f32[2,16,384]{2,0,1:T(2,128)S(1)} %bitcast.79), channel_id=1, source_target_pairs={{0,8},{8,0},{16,24},{24,16},{32,40},{40,32},{48,56},{56,48},{64,72... | collective-permute-start | bytes 147464 | tf_op jit(solution)/shard_map/ppermute | solution.py:130
  44.6 11.3 %all-to-all-done.parts_ref = bf16[32,8,768]{2,1,0:T(8,128)(2,1)S(1)} async-done(((bf16[32,8,768]{2,1,0:T(8,128)(2,1)}), bf16[32,8,768]{2,1,0:T(8,128)(2,1)S(1)}, u32[]{:S(2)}, u32[]{:S(2)}) %all-to-all-start) | async-done | bytes 393248 | tf_op jit(solution)/shard_map/all_to_all | solution.py:139
  56.7 4.2 %all-to-all-start.1 = ((bf16[16,16,768]{2,1,0:T(8,128)(2,1)}), bf16[16,16,768]{2,1,0:T(8,128)(2,1)S(1)}, u32[]{:S(2)}, u32[]{:S(2)}) async-start(bf16[16,16,768]{2,1,0:T(8,128)(2,1)} %shard_map.113), calls=%async_computation.1 | async-start | bytes 786432 | tf_op jit(solution)/shard_map/all_to_all | solution.py:139
  62.3 2.5 %collective-permute-start.5 = (bf16[768,384]{1,0:T(8,128)(2,1)S(1)}, bf16[768,384]{1,0:T(8,128)(2,1)S(1)}, u32[]{:S(2)}, u32[]{:S(2)}) collective-permute-start(bf16[768,384]{1,0:T(8,128)(2,1)S(1)} %add_convert_fusion.a_ref), channel_id=1, source_target_pairs={{0,256},{8,264},{16,272},{24,280},{32,288},{40,296},{48,304},{56,3... | collective-permute-start | bytes 1769480 | tf_op jit(solution)/shard_map/ppermute | solution.py:133
  64.8 13.7 %collective-permute-done.5.b_ref = bf16[768,384]{1,0:T(8,128)(2,1)S(1)} collective-permute-done((bf16[768,384]{1,0:T(8,128)(2,1)S(1)}, bf16[768,384]{1,0:T(8,128)(2,1)S(1)}, u32[]{:S(2)}, u32[]{:S(2)}) %collective-permute-start.5) | collective-permute-done | bytes 589856 | tf_op jit(solution)/shard_map/ppermute | solution.py:133
  79.8 1.9 %collective-permute-start.6 = (bf16[2,768,384]{2,1,0:T(8,128)(2,1)}, bf16[2,768,384]{2,1,0:T(8,128)(2,1)}, u32[]{:S(2)}, u32[]{:S(2)}) collective-permute-start(bf16[2,768,384]{2,1,0:T(8,128)(2,1)} %pad_maximum_fusion.2), channel_id=1, source_target_pairs={{0,8},{8,0},{16,24},{24,16},{32,40},{40,32},{48,56},{56,48},{64,72... | collective-permute-start | bytes 3538952 | tf_op jit(solution)/shard_map/ppermute | solution.py:130
  84.3 6.8 %all-to-all-start.2 = ((bf16[8,16,1536]{2,1,0:T(8,128)(2,1)}), bf16[8,16,1536]{2,1,0:T(8,128)(2,1)S(1)}, u32[]{:S(2)}, u32[]{:S(2)}) async-start(bf16[8,16,1536]{2,1,0:T(8,128)(2,1)} %bitcast.73), calls=%async_computation.2 | async-start | bytes 786432 | tf_op jit(solution)/shard_map/all_to_all | solution.py:139
  91.9 1.9 %collective-permute-start.7 = (bf16[128,1536]{1,0:T(8,128)(2,1)}, bf16[128,1536]{1,0:T(8,128)(2,1)S(1)}, u32[]{:S(2)}, u32[]{:S(2)}) collective-permute-start(bf16[128,1536]{1,0:T(8,128)(2,1)} %shard_map.115.a_ref), channel_id=1, source_target_pairs={{0,256},{8,264},{16,272},{24,280},{32,288},{40,296},{48,304},{56,3... | collective-permute-start | bytes 1179656 | tf_op jit(solution)/shard_map/ppermute | solution.py:133
  93.8 6.9 %all-to-all-done.2 = bf16[8,16,1536]{2,1,0:T(8,128)(2,1)S(1)} async-done(((bf16[8,16,1536]{2,1,0:T(8,128)(2,1)}), bf16[8,16,1536]{2,1,0:T(8,128)(2,1)S(1)}, u32[]{:S(2)}, u32[]{:S(2)}) %all-to-all-start.2) | async-done | bytes 393248 | tf_op jit(solution)/shard_map/all_to_all | solution.py:139
  101.5 3.5 %all-to-all-start.3 = ((bf16[8,16,1536]{2,1,0:T(8,128)(2,1)}), bf16[8,16,1536]{2,1,0:T(8,128)(2,1)S(1)}, u32[]{:S(2)}, u32[]{:S(2)}) async-start(bf16[8,16,1536]{2,1,0:T(8,128)(2,1)} %broadcast_in_dim.23), calls=%async_computation.3 | async-start | bytes 786432 | tf_op jit(solution)/shard_map/all_to_all | solution.py:139
  106.5 7.6 %all-to-all-done.3 = bf16[8,16,1536]{2,1,0:T(8,128)(2,1)S(1)} async-done(((bf16[8,16,1536]{2,1,0:T(8,128)(2,1)}), bf16[8,16,1536]{2,1,0:T(8,128)(2,1)S(1)}, u32[]{:S(2)}, u32[]{:S(2)}) %all-to-all-start.3) | async-done | bytes 393248 | tf_op jit(solution)/shard_map/all_to_all | solution.py:139
  117.3 1.9 %collective-permute-start.8 = (bf16[2,128,1536]{2,1,0:T(8,128)(2,1)S(1)}, bf16[2,128,1536]{2,1,0:T(8,128)(2,1)S(1)}, u32[]{:S(2)}, u32[]{:S(2)}) collective-permute-start(bf16[2,128,1536]{2,1,0:T(8,128)(2,1)S(1)} %shard_map.116.near_ref), channel_id=1, source_target_pairs={{0,8},{8,0},{16,24},{24,16},{32,40},{40,32},{48,56},{56,48},{64,72... | collective-permute-start | bytes 2359304 | tf_op jit(solution)/shard_map/ppermute | solution.py:130
  119.2 12.1 %all-to-all-start.4 = ((bf16[16,8,768]{2,1,0:T(8,128)(2,1)}), bf16[16,8,768]{2,1,0:T(8,128)(2,1)S(1)}, u32[]{:S(2)}, u32[]{:S(2)}) async-start(bf16[16,8,768]{2,1,0:T(8,128)(2,1)} %bitcast.27.after_ref), calls=%async_computation.4 | async-start | bytes 393216 | tf_op jit(solution)/shard_map/all_to_all | solution.py:139
  131.4 1.9 %collective-permute-start.10 = (bf16[128,384]{1,0:T(8,128)(2,1)S(1)}, bf16[128,384]{1,0:T(8,128)(2,1)S(1)}, u32[]{:S(2)}, u32[]{:S(2)}) collective-permute-start(bf16[128,384]{1,0:T(8,128)(2,1)S(1)} %copy-done.9), channel_id=1, source_target_pairs={{0,8},{8,0},{16,24},{24,16},{32,40},{40,32},{48,56},{56,48},{64,72... | collective-permute-start | bytes 294920 | tf_op jit(solution)/shard_map/ppermute | solution.py:130
  133.3 1.9 %collective-permute-start.11 = (bf16[128,384]{1,0:T(8,128)(2,1)S(1)}, bf16[128,384]{1,0:T(8,128)(2,1)S(1)}, u32[]{:S(2)}, u32[]{:S(2)}) collective-permute-start(bf16[128,384]{1,0:T(8,128)(2,1)S(1)} %get-tuple-element.18), channel_id=1, source_target_pairs={{0,264},{8,256},{16,280},{24,272},{32,296},{40,288},{48,312},{56,3... | collective-permute-start | bytes 294920 | tf_op jit(solution)/shard_map/ppermute | solution.py:136
  135.2 4.0 %collective-permute-start.9 = (bf16[128,384]{1,0:T(8,128)(2,1)S(1)}, bf16[128,384]{1,0:T(8,128)(2,1)S(1)}, u32[]{:S(2)}, u32[]{:S(2)}) collective-permute-start(bf16[128,384]{1,0:T(8,128)(2,1)S(1)} %get-tuple-element.16), channel_id=1, source_target_pairs={{0,256},{8,264},{16,272},{24,280},{32,288},{40,296},{48,304},{56,3... | collective-permute-start | bytes 294920 | tf_op jit(solution)/shard_map/ppermute | solution.py:133
  139.3 8.7 %all-to-all-done.4 = bf16[16,8,768]{2,1,0:T(8,128)(2,1)S(1)} async-done(((bf16[16,8,768]{2,1,0:T(8,128)(2,1)}), bf16[16,8,768]{2,1,0:T(8,128)(2,1)S(1)}, u32[]{:S(2)}, u32[]{:S(2)}) %all-to-all-start.4) | async-done | bytes 196640 | tf_op jit(solution)/shard_map/all_to_all | solution.py:139
  148.7 2.3 %shard_map.117 = (bf16[768,384]{1,0:T(8,128)(2,1)}, bf16[384,768]{1,0:T(8,128)(2,1)}) custom-call(s32[2]{0:T(128)S(1)} %pad_add_fusion.at_ref, bf16[2,2,128,384]{3,2,1,0:T(8,128)(2,1)S(1)} %bitcast.69, bf16[128,1536]{1,0:T(8,128)(2,1)S(1)} %bitcast.65, bf16[2,128,1536]{2,1,0:T(8,128)(2,1)S(1)} %shard_map.116.near_ref, ...), custom_call_target="tpu_custom_call" | custom-call | flops 603979776 | bytes 2097152 | tf_op jit(solution)/shard_map/pallas_call | solution.py:248
  (76 shorter events, 26.1 us)
Async XLA Ops:
  0.6 10.3 %copy-start.11 = (s32[512,3]{0,1:T(4,128)S(1)}, s32[512,3]{0,1:T(4,128)}, u32[]{:S(2)}) copy-start(s32[512,3]{0,1:T(4,128)} %param.16) | copy-start | bytes 18436
  5.5 8.2 %copy-start.2 = (bf16[2,256,384]{2,1,0:T(8,128)(2,1)}, bf16[2,256,384]{2,1,0:T(8,128)(2,1)S(1)}, u32[]{:S(2)}) copy-start(bf16[2,256,384]{2,1,0:T(8,128)(2,1)S(1)} %get-tuple-element.12) | copy-start | bytes 1179652
  5.5 23.6 %collective-permute-start.1 = (bf16[384,768]{1,0:T(8,128)(2,1)S(1)}, bf16[384,768]{1,0:T(8,128)(2,1)S(1)}, u32[]{:S(2)}, u32[]{:S(2)}) collective-permute-start(bf16[384,768]{1,0:T(8,128)(2,1)S(1)} %get-tuple-element.13), channel_id=1, source_target_pairs={{0,256},{8,264},{16,272},{24,280},{32,288},{40,296},{48,304},{56,3... | collective-permute-start | bytes 1769480 | tf_op jit(solution)/shard_map/ppermute | solution.py:133
  9.0 3.6 %collective-permute-start = (bf16[256,768]{1,0:T(8,128)(2,1)S(1)}, bf16[256,768]{1,0:T(8,128)(2,1)S(1)}, u32[]{:S(2)}, u32[]{:S(2)}) collective-permute-start(bf16[256,768]{1,0:T(8,128)(2,1)S(1)} %get-tuple-element.14), channel_id=1, source_target_pairs={{0,8},{8,0},{16,24},{24,16},{32,40},{40,32},{48,56},{56,48},{64,72... | collective-permute-start | bytes 1179656 | tf_op jit(solution)/shard_map/ppermute | solution.py:130
  13.8 42.1 %all-to-all-start = ((bf16[32,8,768]{2,1,0:T(8,128)(2,1)}), bf16[32,8,768]{2,1,0:T(8,128)(2,1)S(1)}, u32[]{:S(2)}, u32[]{:S(2)}) async-start(bf16[32,8,768]{2,1,0:T(8,128)(2,1)} %fusion), calls=%async_computation | async-start | bytes 786432 | tf_op jit(solution)/shard_map/all_to_all | solution.py:139
  30.0 11.7 %copy-start.12 = (bf16[8,768]{1,0:T(8,128)(2,1)S(1)}, bf16[8,768]{1,0:T(8,128)(2,1)}, u32[]{:S(2)}) copy-start(bf16[8,768]{1,0:T(8,128)(2,1)} %param.9) | copy-start | bytes 36868
  30.0 13.0 %collective-permute-start.2 = (bf16[2,384,768]{2,1,0:T(8,128)(2,1)S(1)}, bf16[2,384,768]{2,1,0:T(8,128)(2,1)}, u32[]{:S(2)}, u32[]{:S(2)}) collective-permute-start(bf16[2,384,768]{2,1,0:T(8,128)(2,1)S(1)} %pad_maximum_fusion.1), channel_id=1, source_target_pairs={{0,8},{8,0},{16,24},{24,16},{32,40},{40,32},{48,56},{56,48},{64,72... | collective-permute-start | bytes 3538952 | tf_op jit(solution)/shard_map/ppermute | solution.py:130
  33.6 6.1 %collective-permute-start.3 = (f32[2,16,384]{2,1,0:T(8,128)S(1)}, f32[2,16,384]{2,1,0:T(8,128)S(1)}, u32[]{:S(2)}, u32[]{:S(2)}) collective-permute-start(f32[2,16,384]{2,1,0:T(8,128)S(1)} %get-tuple-element.25), channel_id=1, source_target_pairs={{0,256},{8,264},{16,272},{24,280},{32,288},{40,296},{48,304},{56,3... | collective-permute-start | bytes 147464 | tf_op jit(solution)/shard_map/ppermute | solution.py:133
  39.7 3.1 %collective-permute-start.4 = (f32[2,16,384]{2,0,1:T(2,128)S(1)}, f32[2,16,384]{2,0,1:T(2,128)S(1)}, u32[]{:S(2)}, u32[]{:S(2)}) collective-permute-start(f32[2,16,384]{2,0,1:T(2,128)S(1)} %bitcast.79), channel_id=1, source_target_pairs={{0,8},{8,0},{16,24},{24,16},{32,40},{40,32},{48,56},{56,48},{64,72... | collective-permute-start | bytes 147464 | tf_op jit(solution)/shard_map/ppermute | solution.py:130
  42.9 12.9 %copy-start.7 = (bf16[8,768]{1,0:T(8,128)(2,1)S(1)}, bf16[8,768]{1,0:T(8,128)(2,1)}, u32[]{:S(2)}) copy-start(bf16[8,768]{1,0:T(8,128)(2,1)} %teacher_ref.1) | copy-start | bytes 36868
  56.7 26.0 %all-to-all-start.1 = ((bf16[16,16,768]{2,1,0:T(8,128)(2,1)}), bf16[16,16,768]{2,1,0:T(8,128)(2,1)S(1)}, u32[]{:S(2)}, u32[]{:S(2)}) async-start(bf16[16,16,768]{2,1,0:T(8,128)(2,1)} %shard_map.113), calls=%async_computation.1 | async-start | bytes 786432 | tf_op jit(solution)/shard_map/all_to_all | solution.py:139
  62.3 16.2 %collective-permute-start.5 = (bf16[768,384]{1,0:T(8,128)(2,1)S(1)}, bf16[768,384]{1,0:T(8,128)(2,1)S(1)}, u32[]{:S(2)}, u32[]{:S(2)}) collective-permute-start(bf16[768,384]{1,0:T(8,128)(2,1)S(1)} %add_convert_fusion.a_ref), channel_id=1, source_target_pairs={{0,256},{8,264},{16,272},{24,280},{32,288},{40,296},{48,304},{56,3... | collective-permute-start | bytes 1769480 | tf_op jit(solution)/shard_map/ppermute | solution.py:133
  79.8 25.3 %collective-permute-start.6 = (bf16[2,768,384]{2,1,0:T(8,128)(2,1)}, bf16[2,768,384]{2,1,0:T(8,128)(2,1)}, u32[]{:S(2)}, u32[]{:S(2)}) collective-permute-start(bf16[2,768,384]{2,1,0:T(8,128)(2,1)} %pad_maximum_fusion.2), channel_id=1, source_target_pairs={{0,8},{8,0},{16,24},{24,16},{32,40},{40,32},{48,56},{56,48},{64,72... | collective-permute-start | bytes 3538952 | tf_op jit(solution)/shard_map/ppermute | solution.py:130
  84.3 16.4 %all-to-all-start.2 = ((bf16[8,16,1536]{2,1,0:T(8,128)(2,1)}), bf16[8,16,1536]{2,1,0:T(8,128)(2,1)S(1)}, u32[]{:S(2)}, u32[]{:S(2)}) async-start(bf16[8,16,1536]{2,1,0:T(8,128)(2,1)} %bitcast.73), calls=%async_computation.2 | async-start | bytes 786432 | tf_op jit(solution)/shard_map/all_to_all | solution.py:139
  91.9 24.3 %collective-permute-start.7 = (bf16[128,1536]{1,0:T(8,128)(2,1)}, bf16[128,1536]{1,0:T(8,128)(2,1)S(1)}, u32[]{:S(2)}, u32[]{:S(2)}) collective-permute-start(bf16[128,1536]{1,0:T(8,128)(2,1)} %shard_map.115.a_ref), channel_id=1, source_target_pairs={{0,256},{8,264},{16,272},{24,280},{32,288},{40,296},{48,304},{56,3... | collective-permute-start | bytes 1179656 | tf_op jit(solution)/shard_map/ppermute | solution.py:133
  101.5 12.5 %all-to-all-start.3 = ((bf16[8,16,1536]{2,1,0:T(8,128)(2,1)}), bf16[8,16,1536]{2,1,0:T(8,128)(2,1)S(1)}, u32[]{:S(2)}, u32[]{:S(2)}) async-start(bf16[8,16,1536]{2,1,0:T(8,128)(2,1)} %broadcast_in_dim.23), calls=%async_computation.3 | async-start | bytes 786432 | tf_op jit(solution)/shard_map/all_to_all | solution.py:139
  105.0 9.0 %copy-start.1 = (bf16[768,384]{1,0:T(8,128)(2,1)S(1)}, bf16[768,384]{1,0:T(8,128)(2,1)}, u32[]{:S(2)}) copy-start(bf16[768,384]{1,0:T(8,128)(2,1)} %copy-done) | copy-start | bytes 1769476
  116.2 15.2 %copy-start.9 = (bf16[128,384]{1,0:T(8,128)(2,1)S(1)}, bf16[128,384]{1,0:T(8,128)(2,1)}, u32[]{:S(2)}) copy-start(bf16[128,384]{1,0:T(8,128)(2,1)} %copy-done.8) | copy-start | bytes 294916
  116.2 32.5 %copy-start.3 = (bf16[2,256,384]{2,1,0:T(8,128)(2,1)S(1)}, bf16[2,256,384]{2,1,0:T(8,128)(2,1)}, u32[]{:S(2)}) copy-start(bf16[2,256,384]{2,1,0:T(8,128)(2,1)} %copy-done.2) | copy-start | bytes 1179652
  117.3 31.3 %collective-permute-start.8 = (bf16[2,128,1536]{2,1,0:T(8,128)(2,1)S(1)}, bf16[2,128,1536]{2,1,0:T(8,128)(2,1)S(1)}, u32[]{:S(2)}, u32[]{:S(2)}) collective-permute-start(bf16[2,128,1536]{2,1,0:T(8,128)(2,1)S(1)} %shard_map.116.near_ref), channel_id=1, source_target_pairs={{0,8},{8,0},{16,24},{24,16},{32,40},{40,32},{48,56},{56,48},{64,72... | collective-permute-start | bytes 2359304 | tf_op jit(solution)/shard_map/ppermute | solution.py:130
  119.2 28.8 %all-to-all-start.4 = ((bf16[16,8,768]{2,1,0:T(8,128)(2,1)}), bf16[16,8,768]{2,1,0:T(8,128)(2,1)S(1)}, u32[]{:S(2)}, u32[]{:S(2)}) async-start(bf16[16,8,768]{2,1,0:T(8,128)(2,1)} %bitcast.27.after_ref), calls=%async_computation.4 | async-start | bytes 393216 | tf_op jit(solution)/shard_map/all_to_all | solution.py:139
  131.4 17.3 %collective-permute-start.10 = (bf16[128,384]{1,0:T(8,128)(2,1)S(1)}, bf16[128,384]{1,0:T(8,128)(2,1)S(1)}, u32[]{:S(2)}, u32[]{:S(2)}) collective-permute-start(bf16[128,384]{1,0:T(8,128)(2,1)S(1)} %copy-done.9), channel_id=1, source_target_pairs={{0,8},{8,0},{16,24},{24,16},{32,40},{40,32},{48,56},{56,48},{64,72... | collective-permute-start | bytes 294920 | tf_op jit(solution)/shard_map/ppermute | solution.py:130
  133.3 15.3 %collective-permute-start.11 = (bf16[128,384]{1,0:T(8,128)(2,1)S(1)}, bf16[128,384]{1,0:T(8,128)(2,1)S(1)}, u32[]{:S(2)}, u32[]{:S(2)}) collective-permute-start(bf16[128,384]{1,0:T(8,128)(2,1)S(1)} %get-tuple-element.18), channel_id=1, source_target_pairs={{0,264},{8,256},{16,280},{24,272},{32,296},{40,288},{48,312},{56,3... | collective-permute-start | bytes 294920 | tf_op jit(solution)/shard_map/ppermute | solution.py:136
  135.2 13.4 %collective-permute-start.9 = (bf16[128,384]{1,0:T(8,128)(2,1)S(1)}, bf16[128,384]{1,0:T(8,128)(2,1)S(1)}, u32[]{:S(2)}, u32[]{:S(2)}) collective-permute-start(bf16[128,384]{1,0:T(8,128)(2,1)S(1)} %get-tuple-element.16), channel_id=1, source_target_pairs={{0,256},{8,264},{16,272},{24,280},{32,288},{40,296},{48,304},{56,3... | collective-permute-start | bytes 294920 | tf_op jit(solution)/shard_map/ppermute | solution.py:133
  (7 other events, 12.9 us)

commit v4 on v3

--- a/solution.py
+++ b/solution.py
@@ -99,18 +99,24 @@
         ref[...] = one
 
 
-def pair_kernel(a_ref, b_ref, after_ref, pair_ref):
-    pair_ref[0] = a_ref[...]
-    pair_ref[1] = b_ref[...]
-
-
-def grads_kernel(scale, at_ref, act_ref, grad_ref, near_ref, far_ref, y_ref, core_ref, both_ref, first_ref, second_ref):
+def sum_kernel(parts_ref, after_ref, out_ref):
+    total = parts_ref[0].astype(f32)
+    for i in range(1, parts_ref.shape[0]):
+        total += parts_ref[i].astype(f32)
+    out_ref[...] = total.astype(bf16)
+
+
+def later_kernel(a_ref, after_ref, again_ref):
+    again_ref[...] = a_ref[...]
+
+
+def grads_kernel(scale, at_ref, act_ref, grad_ref, *refs):
+    *rows, y_ref, core_ref, both_ref, first_ref, second_ref = refs
     width, model = second_ref.shape
     c, y = at_ref[0], at_ref[1]
     act = [act_ref[c, y], act_ref[c, 1 - y], act_ref[1 - c, y], act_ref[1 - c, 1 - y]]
-    rows = [(ref, i) for ref in (near_ref, far_ref) for i in range(2)]
-    residual = [ref[i, :, :model] for ref, i in rows]
-    features = [ref[i, :, model:] for ref, i in rows]
+    residual = [ref[:, :model] for ref in rows]
+    features = [ref[:, model:] for ref in rows]
     grad = [grad_ref[:, :width]] + [ref[...] for ref in (y_ref, core_ref, both_ref)]
     second = t_dot(jnp.concatenate(act), jnp.concatenate(residual))
     second_ref[...] = (second * scale).astype(bf16)
@@ -235,35 +241,46 @@
             ),
         )(hidden_grad, *[all_in[i] for i in range(4)])
         partial = partial.reshape(zs, quota, model)
-        input_grad = add_up(exchange(partial, "row", along_z)).astype(bf16)
-
-        near_rows = pl.pallas_call(
-            pair_kernel,
-            out_shape=shape(2, group, 2 * model),
-            in_specs=[whole] * 2 + [anywhere],
+        last = exchange(partial, "row", along_z)
+
+        y_rows = from_y(own_rows)
+        later_rows = pl.pallas_call(
+            later_kernel,
+            out_shape=shape(group, 2 * model),
+            in_specs=[whole, anywhere],
             out_specs=whole,
             compiler_params=params,
-            cost_estimate=pl.CostEstimate(flops=0, bytes_accessed=3 * 2**19, transcendentals=0),
-        )(own_rows, from_y(own_rows), partial)
+            cost_estimate=pl.CostEstimate(flops=0, bytes_accessed=2**18, transcendentals=0),
+        )(y_rows, partial)
         first_grad, second_grad = pl.pallas_call(
             functools.partial(grads_kernel, inverse_root),
             out_shape=(shape(model, width), shape(width, model)),
-            in_specs=[scalar] + [whole] * 7,
+            in_specs=[scalar] + [whole] * 9,
             out_specs=(whole,) * 2,
             compiler_params=params,
             cost_estimate=pl.CostEstimate(
-                flops=4 * tokens * width * model, bytes_accessed=2**21, transcendentals=0
+                flops=4 * tokens * width * model, bytes_accessed=2**18, transcendentals=0
             ),
         )(
             jnp.stack([core, y]),
             activated.reshape(2, 2, group, width),
             hidden_grad,
-            near_rows,
-            from_core(near_rows),
+            own_rows,
+            y_rows,
+            from_core(own_rows),
+            from_core(later_rows),
             from_y(for_y),
             from_core(for_core),
             from_both(for_both),
         )
+        input_grad = pl.pallas_call(
+            sum_kernel,
+            out_shape=shape(quota, model),
+            in_specs=[whole, anywhere],
+            out_specs=whole,
+            compiler_params=params,
+            cost_estimate=pl.CostEstimate(flops=2**17, bytes_accessed=2**18, transcendentals=0),
+        )(last, first_grad)
         return (input_grad, first_grad, second_grad)
 
     return local

time: 152 us -> 150 us (0.987)
  the two profiles are of different devices: /device:TPU:32 before, /device:TPU:1 now
where the time goes in v4:
time: 150 us; the launch traced here: 148 us
  starting transfers between devices  75 us (50%)
  waiting for transfers between devices  33.5 us (22%)
  blocking collectives  14.5 us (10%)
  local copies, waits for them, and re-layouts  8.85 us (6%)
  Pallas kernels  7.38 us (5%)
  other arithmetic  5.93 us (4%)
  matrix products  2 us (1%)
    all_to_all x4, starting transfers between devices, exchange(): return lax.all_to_all(a, axis, 0, 0, axis_index_groups=groups, tiled=True)  32.4 us
    ppermute x7, starting transfers between devices, from_core(): return lax.ppermute(a, 'row', swap_core)  25.6 us
    ppermute x5, waiting for transfers between devices, from_y(): return lax.ppermute(a, 'row', swap_y)  16 us
    all_to_all x1, blocking collectives, exchange(): return lax.all_to_all(a, axis, 0, 0, axis_index_groups=groups, tiled=True)  14.5 us
    ppermute x5, starting transfers between devices, from_y(): return lax.ppermute(a, 'row', swap_y)  13.5 us
    all_to_all x4, waiting for transfers between devices, exchange(): return lax.all_to_all(a, axis, 0, 0, axis_index_groups=groups, tiled=True)  12.5 us
    unnamed x28, local copies, waits for them, and re-layouts  5.12 us
    ppermute x1, starting transfers between devices, from_both(): return lax.ppermute(a, 'row', swap_both)  3.54 us
  transfers between devices with their start and end apart: 17, of which 7 were waited for; matrix products, arithmetic and copies ran while one was open for 8% of the time, Pallas kernels for 3%

profile of v4, /device:TPU:1, one launch (start us, length us, event | category | flops | bytes accessed | tf_op | source)
XLA Modules:
  0.0 148.2 jit_solution(2453783209052899454)
XLA Ops:
  5.6 4.0 %collective-permute-start.1 = (bf16[384,768]{1,0:T(8,128)(2,1)S(1)}, bf16[384,768]{1,0:T(8,128)(2,1)S(1)}, u32[]{:S(2)}, u32[]{:S(2)}) collective-permute-start(bf16[384,768]{1,0:T(8,128)(2,1)S(1)} %get-tuple-element.13), channel_id=1, source_target_pairs={{0,256},{8,264},{16,272},{24,280},{32,288},{40,296},{48,304},{56,3... | collective-permute-start | bytes 1769480 | tf_op jit(solution)/shard_map/ppermute | solution.py:139
  9.6 6.7 %collective-permute-start = (bf16[256,768]{1,0:T(8,128)(2,1)S(1)}, bf16[256,768]{1,0:T(8,128)(2,1)S(1)}, u32[]{:S(2)}, u32[]{:S(2)}) collective-permute-start(bf16[256,768]{1,0:T(8,128)(2,1)S(1)} %get-tuple-element.14), channel_id=1, source_target_pairs={{0,8},{8,0},{16,24},{24,16},{32,40},{40,32},{48,56},{56,48},{64,72... | collective-permute-start | bytes 1179656 | tf_op jit(solution)/shard_map/ppermute | solution.py:136
  18.7 11.4 %all-to-all-start = ((bf16[32,8,768]{2,1,0:T(8,128)(2,1)}), bf16[32,8,768]{2,1,0:T(8,128)(2,1)S(1)}, u32[]{:S(2)}, u32[]{:S(2)}) async-start(bf16[32,8,768]{2,1,0:T(8,128)(2,1)} %fusion), calls=%async_computation | async-start | bytes 786432 | tf_op jit(solution)/shard_map/all_to_all | solution.py:145
  31.4 2.7 %collective-permute-start.2 = (bf16[2,384,768]{2,1,0:T(8,128)(2,1)}, bf16[2,384,768]{2,1,0:T(8,128)(2,1)}, u32[]{:S(2)}, u32[]{:S(2)}) collective-permute-start(bf16[2,384,768]{2,1,0:T(8,128)(2,1)} %pad_maximum_fusion.1), channel_id=1, source_target_pairs={{0,8},{8,0},{16,24},{24,16},{32,40},{40,32},{48,56},{56,48},{64,72... | collective-permute-start | bytes 3538952 | tf_op jit(solution)/shard_map/ppermute | solution.py:136
  35.7 3.4 %collective-permute-start.3 = (f32[2,16,384]{2,1,0:T(8,128)S(1)}, f32[2,16,384]{2,1,0:T(8,128)S(1)}, u32[]{:S(2)}, u32[]{:S(2)}) collective-permute-start(f32[2,16,384]{2,1,0:T(8,128)S(1)} %get-tuple-element.25), channel_id=1, source_target_pairs={{0,256},{8,264},{16,272},{24,280},{32,288},{40,296},{48,304},{56,3... | collective-permute-start | bytes 147464 | tf_op jit(solution)/shard_map/ppermute | solution.py:139
  39.2 2.5 %collective-permute-done.3 = f32[2,16,384]{2,1,0:T(8,128)S(1)} collective-permute-done((f32[2,16,384]{2,1,0:T(8,128)S(1)}, f32[2,16,384]{2,1,0:T(8,128)S(1)}, u32[]{:S(2)}, u32[]{:S(2)}) %collective-permute-start.3) | collective-permute-done | bytes 49184 | tf_op jit(solution)/shard_map/ppermute | solution.py:139
  41.7 2.6 %collective-permute-start.4 = (f32[2,16,384]{2,0,1:T(2,128)S(1)}, f32[2,16,384]{2,0,1:T(2,128)S(1)}, u32[]{:S(2)}, u32[]{:S(2)}) collective-permute-start(f32[2,16,384]{2,0,1:T(2,128)S(1)} %bitcast.79), channel_id=1, source_target_pairs={{0,8},{8,0},{16,24},{24,16},{32,40},{40,32},{48,56},{56,48},{64,72... | collective-permute-start | bytes 147464 | tf_op jit(solution)/shard_map/ppermute | solution.py:136
  47.0 8.8 %all-to-all-done.parts_ref = bf16[32,8,768]{2,1,0:T(8,128)(2,1)S(1)} async-done(((bf16[32,8,768]{2,1,0:T(8,128)(2,1)}), bf16[32,8,768]{2,1,0:T(8,128)(2,1)S(1)}, u32[]{:S(2)}, u32[]{:S(2)}) %all-to-all-start) | async-done | bytes 393248 | tf_op jit(solution)/shard_map/all_to_all | solution.py:145
  56.6 4.6 %all-to-all-start.1 = ((bf16[16,16,768]{2,1,0:T(8,128)(2,1)}), bf16[16,16,768]{2,1,0:T(8,128)(2,1)S(1)}, u32[]{:S(2)}, u32[]{:S(2)}) async-start(bf16[16,16,768]{2,1,0:T(8,128)(2,1)} %shard_map.113), calls=%async_computation.1 | async-start | bytes 786432 | tf_op jit(solution)/shard_map/all_to_all | solution.py:145
  62.7 2.1 %collective-permute-start.5 = (bf16[768,384]{1,0:T(8,128)(2,1)S(1)}, bf16[768,384]{1,0:T(8,128)(2,1)S(1)}, u32[]{:S(2)}, u32[]{:S(2)}) collective-permute-start(bf16[768,384]{1,0:T(8,128)(2,1)S(1)} %add_convert_fusion.a_ref), channel_id=1, source_target_pairs={{0,256},{8,264},{16,272},{24,280},{32,288},{40,296},{48,304},{56,3... | collective-permute-start | bytes 1769480 | tf_op jit(solution)/shard_map/ppermute | solution.py:139
  64.8 13.5 %collective-permute-done.5.b_ref = bf16[768,384]{1,0:T(8,128)(2,1)S(1)} collective-permute-done((bf16[768,384]{1,0:T(8,128)(2,1)S(1)}, bf16[768,384]{1,0:T(8,128)(2,1)S(1)}, u32[]{:S(2)}, u32[]{:S(2)}) %collective-permute-start.5) | collective-permute-done | bytes 589856 | tf_op jit(solution)/shard_map/ppermute | solution.py:139
  79.5 3.9 %collective-permute-start.6 = (bf16[2,768,384]{2,1,0:T(8,128)(2,1)}, bf16[2,768,384]{2,1,0:T(8,128)(2,1)}, u32[]{:S(2)}, u32[]{:S(2)}) collective-permute-start(bf16[2,768,384]{2,1,0:T(8,128)(2,1)} %pad_maximum_fusion.2), channel_id=1, source_target_pairs={{0,8},{8,0},{16,24},{24,16},{32,40},{40,32},{48,56},{56,48},{64,72... | collective-permute-start | bytes 3538952 | tf_op jit(solution)/shard_map/ppermute | solution.py:136
  84.4 14.5 %all_to_all.25 = bf16[8,16,1536]{2,1,0:T(8,128)(2,1)S(1)} all-to-all(bf16[8,16,1536]{2,1,0:T(8,128)(2,1)S(1)} %bitcast.73), channel_id=1, replica_groups=mesh['row'=64,'col'=8] {'col'}, dimensions={0} | all-to-all | bytes 786432 | tf_op jit(solution)/shard_map/all_to_all | solution.py:145
  99.7 3.5 %all-to-all-start.3 = ((bf16[8,16,1536]{2,1,0:T(8,128)(2,1)}), bf16[8,16,1536]{2,1,0:T(8,128)(2,1)S(1)}, u32[]{:S(2)}, u32[]{:S(2)}) async-start(bf16[8,16,1536]{2,1,0:T(8,128)(2,1)} %broadcast_in_dim.23), calls=%async_computation.3 | async-start | bytes 786432 | tf_op jit(solution)/shard_map/all_to_all | solution.py:145
  104.0 2.0 %collective-permute-start.7 = (bf16[128,1536]{1,0:T(8,128)(2,1)}, bf16[128,1536]{1,0:T(8,128)(2,1)S(1)}, u32[]{:S(2)}, u32[]{:S(2)}) collective-permute-start(bf16[128,1536]{1,0:T(8,128)(2,1)} %shard_map.115.refs_0_), channel_id=1, source_target_pairs={{0,256},{8,264},{16,272},{24,280},{32,288},{40,296},{48,304},{56,3... | collective-permute-start | bytes 1179656 | tf_op jit(solution)/shard_map/ppermute | solution.py:139
  107.4 3.6 %all-to-all-done.3 = bf16[8,16,1536]{2,1,0:T(8,128)(2,1)S(1)} async-done(((bf16[8,16,1536]{2,1,0:T(8,128)(2,1)}), bf16[8,16,1536]{2,1,0:T(8,128)(2,1)S(1)}, u32[]{:S(2)}, u32[]{:S(2)}) %all-to-all-start.3) | async-done | bytes 393248 | tf_op jit(solution)/shard_map/all_to_all | solution.py:145
  112.5 12.9 %all-to-all-start.4 = ((bf16[16,8,768]{2,1,0:T(8,128)(2,1)}), bf16[16,8,768]{2,1,0:T(8,128)(2,1)S(1)}, u32[]{:S(2)}, u32[]{:S(2)}) async-start(bf16[16,8,768]{2,1,0:T(8,128)(2,1)} %bitcast.27.after_ref), calls=%async_computation.4 | async-start | bytes 393216 | tf_op jit(solution)/shard_map/all_to_all | solution.py:145
  125.4 5.4 %collective-permute-start.8 = (bf16[128,1536]{1,0:T(8,128)(2,1)}, bf16[128,1536]{1,0:T(8,128)(2,1)S(1)}, u32[]{:S(2)}, u32[]{:S(2)}) collective-permute-start(bf16[128,1536]{1,0:T(8,128)(2,1)} %shard_map.115.refs_0_), channel_id=1, source_target_pairs={{0,8},{8,0},{16,24},{24,16},{32,40},{40,32},{48,56},{56,48},{64,72... | collective-permute-start | bytes 1179656 | tf_op jit(solution)/shard_map/ppermute | solution.py:136
  130.8 1.9 %collective-permute-start.9 = (bf16[128,1536]{1,0:T(8,128)(2,1)S(1)}, bf16[128,1536]{1,0:T(8,128)(2,1)S(1)}, u32[]{:S(2)}, u32[]{:S(2)}) collective-permute-start(bf16[128,1536]{1,0:T(8,128)(2,1)S(1)} %shard_map.116), channel_id=1, source_target_pairs={{0,8},{8,0},{16,24},{24,16},{32,40},{40,32},{48,56},{56,48},{64,72... | collective-permute-start | bytes 1179656 | tf_op jit(solution)/shard_map/ppermute | solution.py:136
  132.7 1.9 %collective-permute-start.10 = (bf16[128,384]{1,0:T(8,128)(2,1)S(1)}, bf16[128,384]{1,0:T(8,128)(2,1)S(1)}, u32[]{:S(2)}, u32[]{:S(2)}) collective-permute-start(bf16[128,384]{1,0:T(8,128)(2,1)S(1)} %get-tuple-element.16), channel_id=1, source_target_pairs={{0,256},{8,264},{16,272},{24,280},{32,288},{40,296},{48,304},{56,3... | collective-permute-start | bytes 294920 | tf_op jit(solution)/shard_map/ppermute | solution.py:139
  134.7 2.4 %collective-permute-start.11 = (bf16[128,384]{1,0:T(8,128)(2,1)S(1)}, bf16[128,384]{1,0:T(8,128)(2,1)S(1)}, u32[]{:S(2)}, u32[]{:S(2)}) collective-permute-start(bf16[128,384]{1,0:T(8,128)(2,1)S(1)} %get-tuple-element.17), channel_id=1, source_target_pairs={{0,8},{8,0},{16,24},{24,16},{32,40},{40,32},{48,56},{56,48},{64,72... | collective-permute-start | bytes 294920 | tf_op jit(solution)/shard_map/ppermute | solution.py:136
  137.1 3.5 %collective-permute-start.12 = (bf16[128,384]{1,0:T(8,128)(2,1)S(1)}, bf16[128,384]{1,0:T(8,128)(2,1)S(1)}, u32[]{:S(2)}, u32[]{:S(2)}) collective-permute-start(bf16[128,384]{1,0:T(8,128)(2,1)S(1)} %get-tuple-element.18), channel_id=1, source_target_pairs={{0,264},{8,256},{16,280},{24,272},{32,296},{40,288},{48,312},{56,3... | collective-permute-start | bytes 294920 | tf_op jit(solution)/shard_map/ppermute | solution.py:142
  140.7 3.1 %collective-permute-done.12.refs_6_ = bf16[128,384]{1,0:T(8,128)(2,1)S(1)} collective-permute-done((bf16[128,384]{1,0:T(8,128)(2,1)S(1)}, bf16[128,384]{1,0:T(8,128)(2,1)S(1)}, u32[]{:S(2)}, u32[]{:S(2)}) %collective-permute-start.12) | collective-permute-done | bytes 98336 | tf_op jit(solution)/shard_map/ppermute | solution.py:142
  143.8 2.8 %shard_map.117 = (bf16[768,384]{1,0:T(8,128)(2,1)}, bf16[384,768]{1,0:T(8,128)(2,1)}) custom-call(s32[2]{0:T(128)S(1)} %pad_add_fusion.at_ref, bf16[2,2,128,384]{3,2,1,0:T(8,128)(2,1)S(1)} %bitcast.69, bf16[128,1536]{1,0:T(8,128)(2,1)S(1)} %bitcast.65, bf16[128,1536]{1,0:T(8,128)(2,1)} %shard_map.115.refs_0_, ...), custom_call_target="tpu_custom_call" | custom-call | flops 603979776 | bytes 262144 | tf_op jit(solution)/shard_map/pallas_call | solution.py:255
  (75 shorter events, 23.4 us)
Async XLA Ops:
  0.6 15.7 %copy-start.10 = (s32[512,3]{0,1:T(4,128)S(1)}, s32[512,3]{0,1:T(4,128)}, u32[]{:S(2)}) copy-start(s32[512,3]{0,1:T(4,128)} %param.16) | copy-start | bytes 18436
  5.6 13.2 %copy-start.2 = (bf16[2,256,384]{2,1,0:T(8,128)(2,1)}, bf16[2,256,384]{2,1,0:T(8,128)(2,1)S(1)}, u32[]{:S(2)}) copy-start(bf16[2,256,384]{2,1,0:T(8,128)(2,1)S(1)} %get-tuple-element.12) | copy-start | bytes 1179652
  5.6 24.6 %collective-permute-start.1 = (bf16[384,768]{1,0:T(8,128)(2,1)S(1)}, bf16[384,768]{1,0:T(8,128)(2,1)S(1)}, u32[]{:S(2)}, u32[]{:S(2)}) collective-permute-start(bf16[384,768]{1,0:T(8,128)(2,1)S(1)} %get-tuple-element.13), channel_id=1, source_target_pairs={{0,256},{8,264},{16,272},{24,280},{32,288},{40,296},{48,304},{56,3... | collective-permute-start | bytes 1769480 | tf_op jit(solution)/shard_map/ppermute | solution.py:139
  9.6 8.0 %collective-permute-start = (bf16[256,768]{1,0:T(8,128)(2,1)S(1)}, bf16[256,768]{1,0:T(8,128)(2,1)S(1)}, u32[]{:S(2)}, u32[]{:S(2)}) collective-permute-start(bf16[256,768]{1,0:T(8,128)(2,1)S(1)} %get-tuple-element.14), channel_id=1, source_target_pairs={{0,8},{8,0},{16,24},{24,16},{32,40},{40,32},{48,56},{56,48},{64,72... | collective-permute-start | bytes 1179656 | tf_op jit(solution)/shard_map/ppermute | solution.py:136
  18.7 37.1 %all-to-all-start = ((bf16[32,8,768]{2,1,0:T(8,128)(2,1)}), bf16[32,8,768]{2,1,0:T(8,128)(2,1)S(1)}, u32[]{:S(2)}, u32[]{:S(2)}) async-start(bf16[32,8,768]{2,1,0:T(8,128)(2,1)} %fusion), calls=%async_computation | async-start | bytes 786432 | tf_op jit(solution)/shard_map/all_to_all | solution.py:145
  30.1 15.1 %copy-start.9 = (bf16[384,768]{1,0:T(8,128)(2,1)}, bf16[384,768]{1,0:T(8,128)(2,1)S(1)}, u32[]{:S(2)}) copy-start(bf16[384,768]{1,0:T(8,128)(2,1)S(1)} %collective-permute-done.1) | copy-start | bytes 1769476
  31.4 7.7 %copy-start.12 = (s32[8,6]{1,0:T(8,128)S(1)}, s32[8,6]{1,0:T(8,128)}, u32[]{:S(2)}) copy-start(s32[8,6]{1,0:T(8,128)} %param.10) | copy-start | bytes 580
  31.4 13.0 %copy-start.11 = (bf16[8,768]{1,0:T(8,128)(2,1)S(1)}, bf16[8,768]{1,0:T(8,128)(2,1)}, u32[]{:S(2)}) copy-start(bf16[8,768]{1,0:T(8,128)(2,1)} %param.9) | copy-start | bytes 36868
  31.4 13.9 %collective-permute-start.2 = (bf16[2,384,768]{2,1,0:T(8,128)(2,1)}, bf16[2,384,768]{2,1,0:T(8,128)(2,1)}, u32[]{:S(2)}, u32[]{:S(2)}) collective-permute-start(bf16[2,384,768]{2,1,0:T(8,128)(2,1)} %pad_maximum_fusion.1), channel_id=1, source_target_pairs={{0,8},{8,0},{16,24},{24,16},{32,40},{40,32},{48,56},{56,48},{64,72... | collective-permute-start | bytes 3538952 | tf_op jit(solution)/shard_map/ppermute | solution.py:136
  35.7 6.0 %collective-permute-start.3 = (f32[2,16,384]{2,1,0:T(8,128)S(1)}, f32[2,16,384]{2,1,0:T(8,128)S(1)}, u32[]{:S(2)}, u32[]{:S(2)}) collective-permute-start(f32[2,16,384]{2,1,0:T(8,128)S(1)} %get-tuple-element.25), channel_id=1, source_target_pairs={{0,256},{8,264},{16,272},{24,280},{32,288},{40,296},{48,304},{56,3... | collective-permute-start | bytes 147464 | tf_op jit(solution)/shard_map/ppermute | solution.py:139
  41.7 3.5 %collective-permute-start.4 = (f32[2,16,384]{2,0,1:T(2,128)S(1)}, f32[2,16,384]{2,0,1:T(2,128)S(1)}, u32[]{:S(2)}, u32[]{:S(2)}) collective-permute-start(f32[2,16,384]{2,0,1:T(2,128)S(1)} %bitcast.79), channel_id=1, source_target_pairs={{0,8},{8,0},{16,24},{24,16},{32,40},{40,32},{48,56},{56,48},{64,72... | collective-permute-start | bytes 147464 | tf_op jit(solution)/shard_map/ppermute | solution.py:136
  45.3 10.5 %copy-start.8 = (bf16[8,768]{1,0:T(8,128)(2,1)S(1)}, bf16[8,768]{1,0:T(8,128)(2,1)}, u32[]{:S(2)}) copy-start(bf16[8,768]{1,0:T(8,128)(2,1)} %teacher_ref.1) | copy-start | bytes 36868
  56.6 26.8 %all-to-all-start.1 = ((bf16[16,16,768]{2,1,0:T(8,128)(2,1)}), bf16[16,16,768]{2,1,0:T(8,128)(2,1)S(1)}, u32[]{:S(2)}, u32[]{:S(2)}) async-start(bf16[16,16,768]{2,1,0:T(8,128)(2,1)} %shard_map.113), calls=%async_computation.1 | async-start | bytes 786432 | tf_op jit(solution)/shard_map/all_to_all | solution.py:145
  62.7 15.6 %collective-permute-start.5 = (bf16[768,384]{1,0:T(8,128)(2,1)S(1)}, bf16[768,384]{1,0:T(8,128)(2,1)S(1)}, u32[]{:S(2)}, u32[]{:S(2)}) collective-permute-start(bf16[768,384]{1,0:T(8,128)(2,1)S(1)} %add_convert_fusion.a_ref), channel_id=1, source_target_pairs={{0,256},{8,264},{16,272},{24,280},{32,288},{40,296},{48,304},{56,3... | collective-permute-start | bytes 1769480 | tf_op jit(solution)/shard_map/ppermute | solution.py:139
  79.5 26.5 %collective-permute-start.6 = (bf16[2,768,384]{2,1,0:T(8,128)(2,1)}, bf16[2,768,384]{2,1,0:T(8,128)(2,1)}, u32[]{:S(2)}, u32[]{:S(2)}) collective-permute-start(bf16[2,768,384]{2,1,0:T(8,128)(2,1)} %pad_maximum_fusion.2), channel_id=1, source_target_pairs={{0,8},{8,0},{16,24},{24,16},{32,40},{40,32},{48,56},{56,48},{64,72... | collective-permute-start | bytes 3538952 | tf_op jit(solution)/shard_map/ppermute | solution.py:136
  99.7 11.3 %all-to-all-start.3 = ((bf16[8,16,1536]{2,1,0:T(8,128)(2,1)}), bf16[8,16,1536]{2,1,0:T(8,128)(2,1)S(1)}, u32[]{:S(2)}, u32[]{:S(2)}) async-start(bf16[8,16,1536]{2,1,0:T(8,128)(2,1)} %broadcast_in_dim.23), calls=%async_computation.3 | async-start | bytes 786432 | tf_op jit(solution)/shard_map/all_to_all | solution.py:145
  104.0 26.8 %collective-permute-start.7 = (bf16[128,1536]{1,0:T(8,128)(2,1)}, bf16[128,1536]{1,0:T(8,128)(2,1)S(1)}, u32[]{:S(2)}, u32[]{:S(2)}) collective-permute-start(bf16[128,1536]{1,0:T(8,128)(2,1)} %shard_map.115.refs_0_), channel_id=1, source_target_pairs={{0,256},{8,264},{16,272},{24,280},{32,288},{40,296},{48,304},{56,3... | collective-permute-start | bytes 1179656 | tf_op jit(solution)/shard_map/ppermute | solution.py:139
  112.5 31.3 %copy-start.3 = (bf16[2,256,384]{2,1,0:T(8,128)(2,1)S(1)}, bf16[2,256,384]{2,1,0:T(8,128)(2,1)}, u32[]{:S(2)}) copy-start(bf16[2,256,384]{2,1,0:T(8,128)(2,1)} %copy-done.2) | copy-start | bytes 1179652
  112.5 34.1 %all-to-all-start.4 = ((bf16[16,8,768]{2,1,0:T(8,128)(2,1)}), bf16[16,8,768]{2,1,0:T(8,128)(2,1)S(1)}, u32[]{:S(2)}, u32[]{:S(2)}) async-start(bf16[16,8,768]{2,1,0:T(8,128)(2,1)} %bitcast.27.after_ref), calls=%async_computation.4 | async-start | bytes 393216 | tf_op jit(solution)/shard_map/all_to_all | solution.py:145
  125.4 15.3 %collective-permute-start.8 = (bf16[128,1536]{1,0:T(8,128)(2,1)}, bf16[128,1536]{1,0:T(8,128)(2,1)S(1)}, u32[]{:S(2)}, u32[]{:S(2)}) collective-permute-start(bf16[128,1536]{1,0:T(8,128)(2,1)} %shard_map.115.refs_0_), channel_id=1, source_target_pairs={{0,8},{8,0},{16,24},{24,16},{32,40},{40,32},{48,56},{56,48},{64,72... | collective-permute-start | bytes 1179656 | tf_op jit(solution)/shard_map/ppermute | solution.py:136
  130.8 13.0 %collective-permute-start.9 = (bf16[128,1536]{1,0:T(8,128)(2,1)S(1)}, bf16[128,1536]{1,0:T(8,128)(2,1)S(1)}, u32[]{:S(2)}, u32[]{:S(2)}) collective-permute-start(bf16[128,1536]{1,0:T(8,128)(2,1)S(1)} %shard_map.116), channel_id=1, source_target_pairs={{0,8},{8,0},{16,24},{24,16},{32,40},{40,32},{48,56},{56,48},{64,72... | collective-permute-start | bytes 1179656 | tf_op jit(solution)/shard_map/ppermute | solution.py:136
  132.7 8.0 %collective-permute-start.10 = (bf16[128,384]{1,0:T(8,128)(2,1)S(1)}, bf16[128,384]{1,0:T(8,128)(2,1)S(1)}, u32[]{:S(2)}, u32[]{:S(2)}) collective-permute-start(bf16[128,384]{1,0:T(8,128)(2,1)S(1)} %get-tuple-element.16), channel_id=1, source_target_pairs={{0,256},{8,264},{16,272},{24,280},{32,288},{40,296},{48,304},{56,3... | collective-permute-start | bytes 294920 | tf_op jit(solution)/shard_map/ppermute | solution.py:139
  134.7 6.0 %collective-permute-start.11 = (bf16[128,384]{1,0:T(8,128)(2,1)S(1)}, bf16[128,384]{1,0:T(8,128)(2,1)S(1)}, u32[]{:S(2)}, u32[]{:S(2)}) collective-permute-start(bf16[128,384]{1,0:T(8,128)(2,1)S(1)} %get-tuple-element.17), channel_id=1, source_target_pairs={{0,8},{8,0},{16,24},{24,16},{32,40},{40,32},{48,56},{56,48},{64,72... | collective-permute-start | bytes 294920 | tf_op jit(solution)/shard_map/ppermute | solution.py:136
  137.1 6.7 %collective-permute-start.12 = (bf16[128,384]{1,0:T(8,128)(2,1)S(1)}, bf16[128,384]{1,0:T(8,128)(2,1)S(1)}, u32[]{:S(2)}, u32[]{:S(2)}) collective-permute-start(bf16[128,384]{1,0:T(8,128)(2,1)S(1)} %get-tuple-element.18), channel_id=1, source_target_pairs={{0,264},{8,256},{16,280},{24,272},{32,296},{40,288},{48,312},{56,3... | collective-permute-start | bytes 294920 | tf_op jit(solution)/shard_map/ppermute | solution.py:142
  (6 other events, 12.5 us)

commit v5 on v4

--- a/solution.py
+++ b/solution.py
@@ -111,7 +111,7 @@
 
 
 def grads_kernel(scale, at_ref, act_ref, grad_ref, *refs):
-    *rows, y_ref, core_ref, both_ref, first_ref, second_ref = refs
+    *rows, y_ref, core_ref, both_ref, first_ref, second_ref, done_ref = refs
     width, model = second_ref.shape
     c, y = at_ref[0], at_ref[1]
     act = [act_ref[c, y], act_ref[c, 1 - y], act_ref[1 - c, y], act_ref[1 - c, 1 - y]]
@@ -122,6 +122,7 @@
     second_ref[...] = (second * scale).astype(bf16)
     first = t_dot(jnp.concatenate(features), jnp.concatenate(grad))
     first_ref[...] = (first * scale).astype(bf16)
+    done_ref[...] = jnp.zeros_like(done_ref)
 
 
 def program(rows, cols):
@@ -252,11 +253,11 @@
             compiler_params=params,
             cost_estimate=pl.CostEstimate(flops=0, bytes_accessed=2**18, transcendentals=0),
         )(y_rows, partial)
-        first_grad, second_grad = pl.pallas_call(
+        first_grad, second_grad, done = pl.pallas_call(
             functools.partial(grads_kernel, inverse_root),
-            out_shape=(shape(model, width), shape(width, model)),
+            out_shape=(shape(model, width), shape(width, model), shape(16, 128)),
             in_specs=[scalar] + [whole] * 9,
-            out_specs=(whole,) * 2,
+            out_specs=(whole,) * 3,
             compiler_params=params,
             cost_estimate=pl.CostEstimate(
                 flops=4 * tokens * width * model, bytes_accessed=2**18, transcendentals=0
@@ -280,7 +281,7 @@
             out_specs=whole,
             compiler_params=params,
             cost_estimate=pl.CostEstimate(flops=2**17, bytes_accessed=2**18, transcendentals=0),
-        )(last, first_grad)
+        )(last, done)
         return (input_grad, first_grad, second_grad)
 
     return local

time: 150 us -> 148 us (0.987)
    unnamed x28 -> x26, local copies, waits for them, and re-layouts: 5.12 us -> 4.06 us
where the time goes in v5:
time: 148 us; the launch traced here: 147 us
  starting transfers between devices  75 us (51%)
  waiting for transfers between devices  33.5 us (23%)
  blocking collectives  14.5 us (10%)
  local copies, waits for them, and re-layouts  7.79 us (5%)
  Pallas kernels  7.38 us (5%)
  other arithmetic  5.91 us (4%)
  matrix products  2.01 us (1%)
    all_to_all x4, starting transfers between devices, exchange(): return lax.all_to_all(a, axis, 0, 0, axis_index_groups=groups, tiled=True)  32.4 us
    ppermute x7, starting transfers between devices, from_core(): return lax.ppermute(a, 'row', swap_core)  25.6 us
    ppermute x5, waiting for transfers between devices, from_y(): return lax.ppermute(a, 'row', swap_y)  16 us
    all_to_all x1, blocking collectives, exchange(): return lax.all_to_all(a, axis, 0, 0, axis_index_groups=groups, tiled=True)  14.5 us
    ppermute x5, starting transfers between devices, from_y(): return lax.ppermute(a, 'row', swap_y)  13.5 us
    all_to_all x4, waiting for transfers between devices, exchange(): return lax.all_to_all(a, axis, 0, 0, axis_index_groups=groups, tiled=True)  12.4 us
    unnamed x26, local copies, waits for them, and re-layouts  4.06 us
    ppermute x1, starting transfers between devices, from_both(): return lax.ppermute(a, 'row', swap_both)  3.54 us
  transfers between devices with their start and end apart: 17, of which 7 were waited for; matrix products, arithmetic and copies ran while one was open for 8% of the time, Pallas kernels for 3%

profile of v5, /device:TPU:1, one launch (start us, length us, event | category | flops | bytes accessed | tf_op | source)
XLA Modules:
  0.0 147.2 jit_solution(15512651179418212918)
XLA Ops:
  5.6 4.0 %collective-permute-start.1 = (bf16[384,768]{1,0:T(8,128)(2,1)S(1)}, bf16[384,768]{1,0:T(8,128)(2,1)S(1)}, u32[]{:S(2)}, u32[]{:S(2)}) collective-permute-start(bf16[384,768]{1,0:T(8,128)(2,1)S(1)} %get-tuple-element.14), channel_id=1, source_target_pairs={{0,256},{8,264},{16,272},{24,280},{32,288},{40,296},{48,304},{56,3... | collective-permute-start | bytes 1769480 | tf_op jit(solution)/shard_map/ppermute | solution.py:140
  9.6 6.7 %collective-permute-start = (bf16[256,768]{1,0:T(8,128)(2,1)S(1)}, bf16[256,768]{1,0:T(8,128)(2,1)S(1)}, u32[]{:S(2)}, u32[]{:S(2)}) collective-permute-start(bf16[256,768]{1,0:T(8,128)(2,1)S(1)} %get-tuple-element.15), channel_id=1, source_target_pairs={{0,8},{8,0},{16,24},{24,16},{32,40},{40,32},{48,56},{56,48},{64,72... | collective-permute-start | bytes 1179656 | tf_op jit(solution)/shard_map/ppermute | solution.py:137
  18.7 11.4 %all-to-all-start = ((bf16[32,8,768]{2,1,0:T(8,128)(2,1)}), bf16[32,8,768]{2,1,0:T(8,128)(2,1)S(1)}, u32[]{:S(2)}, u32[]{:S(2)}) async-start(bf16[32,8,768]{2,1,0:T(8,128)(2,1)} %fusion), calls=%async_computation | async-start | bytes 786432 | tf_op jit(solution)/shard_map/all_to_all | solution.py:146
  31.4 2.7 %collective-permute-start.2 = (bf16[2,384,768]{2,1,0:T(8,128)(2,1)}, bf16[2,384,768]{2,1,0:T(8,128)(2,1)}, u32[]{:S(2)}, u32[]{:S(2)}) collective-permute-start(bf16[2,384,768]{2,1,0:T(8,128)(2,1)} %pad_maximum_fusion.1), channel_id=1, source_target_pairs={{0,8},{8,0},{16,24},{24,16},{32,40},{40,32},{48,56},{56,48},{64,72... | collective-permute-start | bytes 3538952 | tf_op jit(solution)/shard_map/ppermute | solution.py:137
  35.7 3.4 %collective-permute-start.3 = (f32[2,16,384]{2,1,0:T(8,128)S(1)}, f32[2,16,384]{2,1,0:T(8,128)S(1)}, u32[]{:S(2)}, u32[]{:S(2)}) collective-permute-start(f32[2,16,384]{2,1,0:T(8,128)S(1)} %get-tuple-element.27), channel_id=1, source_target_pairs={{0,256},{8,264},{16,272},{24,280},{32,288},{40,296},{48,304},{56,3... | collective-permute-start | bytes 147464 | tf_op jit(solution)/shard_map/ppermute | solution.py:140
  39.2 2.5 %collective-permute-done.3 = f32[2,16,384]{2,1,0:T(8,128)S(1)} collective-permute-done((f32[2,16,384]{2,1,0:T(8,128)S(1)}, f32[2,16,384]{2,1,0:T(8,128)S(1)}, u32[]{:S(2)}, u32[]{:S(2)}) %collective-permute-start.3) | collective-permute-done | bytes 49184 | tf_op jit(solution)/shard_map/ppermute | solution.py:140
  41.8 2.6 %collective-permute-start.4 = (f32[2,16,384]{2,0,1:T(2,128)S(1)}, f32[2,16,384]{2,0,1:T(2,128)S(1)}, u32[]{:S(2)}, u32[]{:S(2)}) collective-permute-start(f32[2,16,384]{2,0,1:T(2,128)S(1)} %bitcast.79), channel_id=1, source_target_pairs={{0,8},{8,0},{16,24},{24,16},{32,40},{40,32},{48,56},{56,48},{64,72... | collective-permute-start | bytes 147464 | tf_op jit(solution)/shard_map/ppermute | solution.py:137
  47.0 8.8 %all-to-all-done.parts_ref = bf16[32,8,768]{2,1,0:T(8,128)(2,1)S(1)} async-done(((bf16[32,8,768]{2,1,0:T(8,128)(2,1)}), bf16[32,8,768]{2,1,0:T(8,128)(2,1)S(1)}, u32[]{:S(2)}, u32[]{:S(2)}) %all-to-all-start) | async-done | bytes 393248 | tf_op jit(solution)/shard_map/all_to_all | solution.py:146
  56.6 4.6 %all-to-all-start.1 = ((bf16[16,16,768]{2,1,0:T(8,128)(2,1)}), bf16[16,16,768]{2,1,0:T(8,128)(2,1)S(1)}, u32[]{:S(2)}, u32[]{:S(2)}) async-start(bf16[16,16,768]{2,1,0:T(8,128)(2,1)} %shard_map.113), calls=%async_computation.1 | async-start | bytes 786432 | tf_op jit(solution)/shard_map/all_to_all | solution.py:146
  62.7 2.1 %collective-permute-start.5 = (bf16[768,384]{1,0:T(8,128)(2,1)S(1)}, bf16[768,384]{1,0:T(8,128)(2,1)S(1)}, u32[]{:S(2)}, u32[]{:S(2)}) collective-permute-start(bf16[768,384]{1,0:T(8,128)(2,1)S(1)} %add_convert_fusion.a_ref), channel_id=1, source_target_pairs={{0,256},{8,264},{16,272},{24,280},{32,288},{40,296},{48,304},{56,3... | collective-permute-start | bytes 1769480 | tf_op jit(solution)/shard_map/ppermute | solution.py:140
  64.8 13.5 %collective-permute-done.5.b_ref = bf16[768,384]{1,0:T(8,128)(2,1)S(1)} collective-permute-done((bf16[768,384]{1,0:T(8,128)(2,1)S(1)}, bf16[768,384]{1,0:T(8,128)(2,1)S(1)}, u32[]{:S(2)}, u32[]{:S(2)}) %collective-permute-start.5) | collective-permute-done | bytes 589856 | tf_op jit(solution)/shard_map/ppermute | solution.py:140
  79.5 3.9 %collective-permute-start.6 = (bf16[2,768,384]{2,1,0:T(8,128)(2,1)}, bf16[2,768,384]{2,1,0:T(8,128)(2,1)}, u32[]{:S(2)}, u32[]{:S(2)}) collective-permute-start(bf16[2,768,384]{2,1,0:T(8,128)(2,1)} %pad_maximum_fusion.2), channel_id=1, source_target_pairs={{0,8},{8,0},{16,24},{24,16},{32,40},{40,32},{48,56},{56,48},{64,72... | collective-permute-start | bytes 3538952 | tf_op jit(solution)/shard_map/ppermute | solution.py:137
  84.4 14.5 %all_to_all.25 = bf16[8,16,1536]{2,1,0:T(8,128)(2,1)S(1)} all-to-all(bf16[8,16,1536]{2,1,0:T(8,128)(2,1)S(1)} %bitcast.73), channel_id=1, replica_groups=mesh['row'=64,'col'=8] {'col'}, dimensions={0} | all-to-all | bytes 786432 | tf_op jit(solution)/shard_map/all_to_all | solution.py:146
  99.7 3.5 %all-to-all-start.3 = ((bf16[8,16,1536]{2,1,0:T(8,128)(2,1)}), bf16[8,16,1536]{2,1,0:T(8,128)(2,1)S(1)}, u32[]{:S(2)}, u32[]{:S(2)}) async-start(bf16[8,16,1536]{2,1,0:T(8,128)(2,1)} %broadcast_in_dim.23), calls=%async_computation.3 | async-start | bytes 786432 | tf_op jit(solution)/shard_map/all_to_all | solution.py:146
  104.0 2.0 %collective-permute-start.7 = (bf16[128,1536]{1,0:T(8,128)(2,1)}, bf16[128,1536]{1,0:T(8,128)(2,1)S(1)}, u32[]{:S(2)}, u32[]{:S(2)}) collective-permute-start(bf16[128,1536]{1,0:T(8,128)(2,1)} %shard_map.115.refs_0_), channel_id=1, source_target_pairs={{0,256},{8,264},{16,272},{24,280},{32,288},{40,296},{48,304},{56,3... | collective-permute-start | bytes 1179656 | tf_op jit(solution)/shard_map/ppermute | solution.py:140
  107.4 3.6 %all-to-all-done.3 = bf16[8,16,1536]{2,1,0:T(8,128)(2,1)S(1)} async-done(((bf16[8,16,1536]{2,1,0:T(8,128)(2,1)}), bf16[8,16,1536]{2,1,0:T(8,128)(2,1)S(1)}, u32[]{:S(2)}, u32[]{:S(2)}) %all-to-all-start.3) | async-done | bytes 393248 | tf_op jit(solution)/shard_map/all_to_all | solution.py:146
  112.5 12.9 %all-to-all-start.4 = ((bf16[16,8,768]{2,1,0:T(8,128)(2,1)}), bf16[16,8,768]{2,1,0:T(8,128)(2,1)S(1)}, u32[]{:S(2)}, u32[]{:S(2)}) async-start(bf16[16,8,768]{2,1,0:T(8,128)(2,1)} %bitcast.27.after_ref), calls=%async_computation.4 | async-start | bytes 393216 | tf_op jit(solution)/shard_map/all_to_all | solution.py:146
  125.4 5.4 %collective-permute-start.8 = (bf16[128,1536]{1,0:T(8,128)(2,1)}, bf16[128,1536]{1,0:T(8,128)(2,1)S(1)}, u32[]{:S(2)}, u32[]{:S(2)}) collective-permute-start(bf16[128,1536]{1,0:T(8,128)(2,1)} %shard_map.115.refs_0_), channel_id=1, source_target_pairs={{0,8},{8,0},{16,24},{24,16},{32,40},{40,32},{48,56},{56,48},{64,72... | collective-permute-start | bytes 1179656 | tf_op jit(solution)/shard_map/ppermute | solution.py:137
  130.8 1.9 %collective-permute-start.9 = (bf16[128,1536]{1,0:T(8,128)(2,1)S(1)}, bf16[128,1536]{1,0:T(8,128)(2,1)S(1)}, u32[]{:S(2)}, u32[]{:S(2)}) collective-permute-start(bf16[128,1536]{1,0:T(8,128)(2,1)S(1)} %shard_map.116), channel_id=1, source_target_pairs={{0,8},{8,0},{16,24},{24,16},{32,40},{40,32},{48,56},{56,48},{64,72... | collective-permute-start | bytes 1179656 | tf_op jit(solution)/shard_map/ppermute | solution.py:137
  132.7 1.9 %collective-permute-start.10 = (bf16[128,384]{1,0:T(8,128)(2,1)S(1)}, bf16[128,384]{1,0:T(8,128)(2,1)S(1)}, u32[]{:S(2)}, u32[]{:S(2)}) collective-permute-start(bf16[128,384]{1,0:T(8,128)(2,1)S(1)} %get-tuple-element.17), channel_id=1, source_target_pairs={{0,256},{8,264},{16,272},{24,280},{32,288},{40,296},{48,304},{56,3... | collective-permute-start | bytes 294920 | tf_op jit(solution)/shard_map/ppermute | solution.py:140
  134.7 2.4 %collective-permute-start.11 = (bf16[128,384]{1,0:T(8,128)(2,1)S(1)}, bf16[128,384]{1,0:T(8,128)(2,1)S(1)}, u32[]{:S(2)}, u32[]{:S(2)}) collective-permute-start(bf16[128,384]{1,0:T(8,128)(2,1)S(1)} %get-tuple-element.18), channel_id=1, source_target_pairs={{0,8},{8,0},{16,24},{24,16},{32,40},{40,32},{48,56},{56,48},{64,72... | collective-permute-start | bytes 294920 | tf_op jit(solution)/shard_map/ppermute | solution.py:137
  137.1 3.5 %collective-permute-start.12 = (bf16[128,384]{1,0:T(8,128)(2,1)S(1)}, bf16[128,384]{1,0:T(8,128)(2,1)S(1)}, u32[]{:S(2)}, u32[]{:S(2)}) collective-permute-start(bf16[128,384]{1,0:T(8,128)(2,1)S(1)} %get-tuple-element.19), channel_id=1, source_target_pairs={{0,264},{8,256},{16,280},{24,272},{32,296},{40,288},{48,312},{56,3... | collective-permute-start | bytes 294920 | tf_op jit(solution)/shard_map/ppermute | solution.py:143
  140.7 3.1 %collective-permute-done.12.refs_6_ = bf16[128,384]{1,0:T(8,128)(2,1)S(1)} collective-permute-done((bf16[128,384]{1,0:T(8,128)(2,1)S(1)}, bf16[128,384]{1,0:T(8,128)(2,1)S(1)}, u32[]{:S(2)}, u32[]{:S(2)}) %collective-permute-start.12) | collective-permute-done | bytes 98336 | tf_op jit(solution)/shard_map/ppermute | solution.py:143
  143.8 2.8 %shard_map.117 = (bf16[768,384]{1,0:T(8,128)(2,1)}, bf16[384,768]{1,0:T(8,128)(2,1)}, bf16[16,128]{1,0:T(8,128)(2,1)S(1)}) custom-call(s32[2]{0:T(128)S(1)} %pad_add_fusion.at_ref, bf16[2,2,128,384]{3,2,1,0:T(8,128)(2,1)S(1)} %bitcast.69, bf16[128,1536]{1,0:T(8,128)(2,1)S(1)} %bitcast.65, bf16[128,1536]{1,0:T(8,128)(2,1)} %shard_map.115.refs_0_, ...), custom_call_target="tpu_custom_call" | custom-call | flops 603979776 | bytes 262144 | tf_op jit(solution)/shard_map/pallas_call | solution.py:256
  (73 shorter events, 22.3 us)
Async XLA Ops:
  0.6 15.7 %copy-start.9 = (s32[512,3]{0,1:T(4,128)S(1)}, s32[512,3]{0,1:T(4,128)}, u32[]{:S(2)}) copy-start(s32[512,3]{0,1:T(4,128)} %param.16) | copy-start | bytes 18436
  5.6 13.2 %copy-start.2 = (bf16[2,256,384]{2,1,0:T(8,128)(2,1)}, bf16[2,256,384]{2,1,0:T(8,128)(2,1)S(1)}, u32[]{:S(2)}) copy-start(bf16[2,256,384]{2,1,0:T(8,128)(2,1)S(1)} %get-tuple-element.13) | copy-start | bytes 1179652
  5.6 24.6 %collective-permute-start.1 = (bf16[384,768]{1,0:T(8,128)(2,1)S(1)}, bf16[384,768]{1,0:T(8,128)(2,1)S(1)}, u32[]{:S(2)}, u32[]{:S(2)}) collective-permute-start(bf16[384,768]{1,0:T(8,128)(2,1)S(1)} %get-tuple-element.14), channel_id=1, source_target_pairs={{0,256},{8,264},{16,272},{24,280},{32,288},{40,296},{48,304},{56,3... | collective-permute-start | bytes 1769480 | tf_op jit(solution)/shard_map/ppermute | solution.py:140
  9.6 8.0 %collective-permute-start = (bf16[256,768]{1,0:T(8,128)(2,1)S(1)}, bf16[256,768]{1,0:T(8,128)(2,1)S(1)}, u32[]{:S(2)}, u32[]{:S(2)}) collective-permute-start(bf16[256,768]{1,0:T(8,128)(2,1)S(1)} %get-tuple-element.15), channel_id=1, source_target_pairs={{0,8},{8,0},{16,24},{24,16},{32,40},{40,32},{48,56},{56,48},{64,72... | collective-permute-start | bytes 1179656 | tf_op jit(solution)/shard_map/ppermute | solution.py:137
  18.7 37.1 %all-to-all-start = ((bf16[32,8,768]{2,1,0:T(8,128)(2,1)}), bf16[32,8,768]{2,1,0:T(8,128)(2,1)S(1)}, u32[]{:S(2)}, u32[]{:S(2)}) async-start(bf16[32,8,768]{2,1,0:T(8,128)(2,1)} %fusion), calls=%async_computation | async-start | bytes 786432 | tf_op jit(solution)/shard_map/all_to_all | solution.py:146
  30.1 15.1 %copy-start.8 = (bf16[384,768]{1,0:T(8,128)(2,1)}, bf16[384,768]{1,0:T(8,128)(2,1)S(1)}, u32[]{:S(2)}) copy-start(bf16[384,768]{1,0:T(8,128)(2,1)S(1)} %collective-permute-done.1) | copy-start | bytes 1769476
  31.4 7.7 %copy-start.11 = (s32[8,6]{1,0:T(8,128)S(1)}, s32[8,6]{1,0:T(8,128)}, u32[]{:S(2)}) copy-start(s32[8,6]{1,0:T(8,128)} %param.10) | copy-start | bytes 580
  31.4 13.0 %copy-start.10 = (bf16[8,768]{1,0:T(8,128)(2,1)S(1)}, bf16[8,768]{1,0:T(8,128)(2,1)}, u32[]{:S(2)}) copy-start(bf16[8,768]{1,0:T(8,128)(2,1)} %param.9) | copy-start | bytes 36868
  31.4 13.9 %collective-permute-start.2 = (bf16[2,384,768]{2,1,0:T(8,128)(2,1)}, bf16[2,384,768]{2,1,0:T(8,128)(2,1)}, u32[]{:S(2)}, u32[]{:S(2)}) collective-permute-start(bf16[2,384,768]{2,1,0:T(8,128)(2,1)} %pad_maximum_fusion.1), channel_id=1, source_target_pairs={{0,8},{8,0},{16,24},{24,16},{32,40},{40,32},{48,56},{56,48},{64,72... | collective-permute-start | bytes 3538952 | tf_op jit(solution)/shard_map/ppermute | solution.py:137
  35.7 6.1 %collective-permute-start.3 = (f32[2,16,384]{2,1,0:T(8,128)S(1)}, f32[2,16,384]{2,1,0:T(8,128)S(1)}, u32[]{:S(2)}, u32[]{:S(2)}) collective-permute-start(f32[2,16,384]{2,1,0:T(8,128)S(1)} %get-tuple-element.27), channel_id=1, source_target_pairs={{0,256},{8,264},{16,272},{24,280},{32,288},{40,296},{48,304},{56,3... | collective-permute-start | bytes 147464 | tf_op jit(solution)/shard_map/ppermute | solution.py:140
  41.8 3.5 %collective-permute-start.4 = (f32[2,16,384]{2,0,1:T(2,128)S(1)}, f32[2,16,384]{2,0,1:T(2,128)S(1)}, u32[]{:S(2)}, u32[]{:S(2)}) collective-permute-start(f32[2,16,384]{2,0,1:T(2,128)S(1)} %bitcast.79), channel_id=1, source_target_pairs={{0,8},{8,0},{16,24},{24,16},{32,40},{40,32},{48,56},{56,48},{64,72... | collective-permute-start | bytes 147464 | tf_op jit(solution)/shard_map/ppermute | solution.py:137
  45.3 10.5 %copy-start.7 = (bf16[8,768]{1,0:T(8,128)(2,1)S(1)}, bf16[8,768]{1,0:T(8,128)(2,1)}, u32[]{:S(2)}) copy-start(bf16[8,768]{1,0:T(8,128)(2,1)} %teacher_ref.1) | copy-start | bytes 36868
  56.6 26.8 %all-to-all-start.1 = ((bf16[16,16,768]{2,1,0:T(8,128)(2,1)}), bf16[16,16,768]{2,1,0:T(8,128)(2,1)S(1)}, u32[]{:S(2)}, u32[]{:S(2)}) async-start(bf16[16,16,768]{2,1,0:T(8,128)(2,1)} %shard_map.113), calls=%async_computation.1 | async-start | bytes 786432 | tf_op jit(solution)/shard_map/all_to_all | solution.py:146
  62.7 15.6 %collective-permute-start.5 = (bf16[768,384]{1,0:T(8,128)(2,1)S(1)}, bf16[768,384]{1,0:T(8,128)(2,1)S(1)}, u32[]{:S(2)}, u32[]{:S(2)}) collective-permute-start(bf16[768,384]{1,0:T(8,128)(2,1)S(1)} %add_convert_fusion.a_ref), channel_id=1, source_target_pairs={{0,256},{8,264},{16,272},{24,280},{32,288},{40,296},{48,304},{56,3... | collective-permute-start | bytes 1769480 | tf_op jit(solution)/shard_map/ppermute | solution.py:140
  79.5 26.5 %collective-permute-start.6 = (bf16[2,768,384]{2,1,0:T(8,128)(2,1)}, bf16[2,768,384]{2,1,0:T(8,128)(2,1)}, u32[]{:S(2)}, u32[]{:S(2)}) collective-permute-start(bf16[2,768,384]{2,1,0:T(8,128)(2,1)} %pad_maximum_fusion.2), channel_id=1, source_target_pairs={{0,8},{8,0},{16,24},{24,16},{32,40},{40,32},{48,56},{56,48},{64,72... | collective-permute-start | bytes 3538952 | tf_op jit(solution)/shard_map/ppermute | solution.py:137
  99.7 11.3 %all-to-all-start.3 = ((bf16[8,16,1536]{2,1,0:T(8,128)(2,1)}), bf16[8,16,1536]{2,1,0:T(8,128)(2,1)S(1)}, u32[]{:S(2)}, u32[]{:S(2)}) async-start(bf16[8,16,1536]{2,1,0:T(8,128)(2,1)} %broadcast_in_dim.23), calls=%async_computation.3 | async-start | bytes 786432 | tf_op jit(solution)/shard_map/all_to_all | solution.py:146
  104.0 26.8 %collective-permute-start.7 = (bf16[128,1536]{1,0:T(8,128)(2,1)}, bf16[128,1536]{1,0:T(8,128)(2,1)S(1)}, u32[]{:S(2)}, u32[]{:S(2)}) collective-permute-start(bf16[128,1536]{1,0:T(8,128)(2,1)} %shard_map.115.refs_0_), channel_id=1, source_target_pairs={{0,256},{8,264},{16,272},{24,280},{32,288},{40,296},{48,304},{56,3... | collective-permute-start | bytes 1179656 | tf_op jit(solution)/shard_map/ppermute | solution.py:140
  112.5 31.3 %copy-start.3 = (bf16[2,256,384]{2,1,0:T(8,128)(2,1)S(1)}, bf16[2,256,384]{2,1,0:T(8,128)(2,1)}, u32[]{:S(2)}) copy-start(bf16[2,256,384]{2,1,0:T(8,128)(2,1)} %copy-done.2) | copy-start | bytes 1179652
  112.5 34.1 %all-to-all-start.4 = ((bf16[16,8,768]{2,1,0:T(8,128)(2,1)}), bf16[16,8,768]{2,1,0:T(8,128)(2,1)S(1)}, u32[]{:S(2)}, u32[]{:S(2)}) async-start(bf16[16,8,768]{2,1,0:T(8,128)(2,1)} %bitcast.27.after_ref), calls=%async_computation.4 | async-start | bytes 393216 | tf_op jit(solution)/shard_map/all_to_all | solution.py:146
  125.4 15.3 %collective-permute-start.8 = (bf16[128,1536]{1,0:T(8,128)(2,1)}, bf16[128,1536]{1,0:T(8,128)(2,1)S(1)}, u32[]{:S(2)}, u32[]{:S(2)}) collective-permute-start(bf16[128,1536]{1,0:T(8,128)(2,1)} %shard_map.115.refs_0_), channel_id=1, source_target_pairs={{0,8},{8,0},{16,24},{24,16},{32,40},{40,32},{48,56},{56,48},{64,72... | collective-permute-start | bytes 1179656 | tf_op jit(solution)/shard_map/ppermute | solution.py:137
  130.8 13.0 %collective-permute-start.9 = (bf16[128,1536]{1,0:T(8,128)(2,1)S(1)}, bf16[128,1536]{1,0:T(8,128)(2,1)S(1)}, u32[]{:S(2)}, u32[]{:S(2)}) collective-permute-start(bf16[128,1536]{1,0:T(8,128)(2,1)S(1)} %shard_map.116), channel_id=1, source_target_pairs={{0,8},{8,0},{16,24},{24,16},{32,40},{40,32},{48,56},{56,48},{64,72... | collective-permute-start | bytes 1179656 | tf_op jit(solution)/shard_map/ppermute | solution.py:137
  132.7 8.0 %collective-permute-start.10 = (bf16[128,384]{1,0:T(8,128)(2,1)S(1)}, bf16[128,384]{1,0:T(8,128)(2,1)S(1)}, u32[]{:S(2)}, u32[]{:S(2)}) collective-permute-start(bf16[128,384]{1,0:T(8,128)(2,1)S(1)} %get-tuple-element.17), channel_id=1, source_target_pairs={{0,256},{8,264},{16,272},{24,280},{32,288},{40,296},{48,304},{56,3... | collective-permute-start | bytes 294920 | tf_op jit(solution)/shard_map/ppermute | solution.py:140
  134.7 6.0 %collective-permute-start.11 = (bf16[128,384]{1,0:T(8,128)(2,1)S(1)}, bf16[128,384]{1,0:T(8,128)(2,1)S(1)}, u32[]{:S(2)}, u32[]{:S(2)}) collective-permute-start(bf16[128,384]{1,0:T(8,128)(2,1)S(1)} %get-tuple-element.18), channel_id=1, source_target_pairs={{0,8},{8,0},{16,24},{24,16},{32,40},{40,32},{48,56},{56,48},{64,72... | collective-permute-start | bytes 294920 | tf_op jit(solution)/shard_map/ppermute | solution.py:137
  137.1 6.7 %collective-permute-start.12 = (bf16[128,384]{1,0:T(8,128)(2,1)S(1)}, bf16[128,384]{1,0:T(8,128)(2,1)S(1)}, u32[]{:S(2)}, u32[]{:S(2)}) collective-permute-start(bf16[128,384]{1,0:T(8,128)(2,1)S(1)} %get-tuple-element.19), channel_id=1, source_target_pairs={{0,264},{8,256},{16,280},{24,272},{32,296},{40,288},{48,312},{56,3... | collective-permute-start | bytes 294920 | tf_op jit(solution)/shard_map/ppermute | solution.py:143
  (5 other events, 11.4 us)

commit v6 on v5

--- a/solution.py
+++ b/solution.py
@@ -196,7 +196,7 @@
         parts = exchange(both, "row", same_core)
 
         all_out = of_four(noisy_out).reshape(4 * width, model)
-        all_in = of_four(noisy_in)
+        in_y = from_y(noisy_in)
         place = lax.axis_index("col")
         own = pick(preactivation.reshape(2, cols, 2 * share, width).swapaxes(0, 1), place)
         own_mask = pick(adc_mask.reshape(2, cols, 2 * share, -1).swapaxes(0, 1), place)
@@ -223,6 +223,14 @@
         own_grad = (add_up(exchange(fresh, "col")) * slope).astype(bf16)
         hidden_grad = spread(own_grad, cols, "col").reshape(group, 4 * width)
 
+        later_in = pl.pallas_call(
+            later_kernel,
+            out_shape=shape(model, width),
+            in_specs=[whole, anywhere],
+            out_specs=whole,
+            compiler_params=params,
+            cost_estimate=pl.CostEstimate(flops=0, bytes_accessed=2**18, transcendentals=0),
+        )(in_y, fresh)
         own_rows = pl.pallas_call(
             rows_kernel,
             out_shape=shape(group, 2 * model),
@@ -240,7 +248,7 @@
             cost_estimate=pl.CostEstimate(
                 flops=8 * group * width * model, bytes_accessed=3 * 2**20, transcendentals=0
             ),
-        )(hidden_grad, *[all_in[i] for i in range(4)])
+        )(hidden_grad, noisy_in, in_y, from_core(noisy_in), from_core(later_in))
         partial = partial.reshape(zs, quota, model)
         last = exchange(partial, "row", along_z)
 

time: 148 us -> 146 us (0.986)
  blocking collectives: 14.5 us -> 0 us
  starting transfers between devices: 75 us -> 83 us
  waiting for transfers between devices: 33.5 us -> 37.8 us
    all_to_all x4 -> x5, waiting for transfers between devices: 12.4 us -> 30.5 us  [exchange(): return lax.all_to_all(a, axis, 0, 0, axis_index_groups=groups, tiled=True)]
    all_to_all x1 -> x0, blocking collectives: 14.5 us -> none  [exchange(): return lax.all_to_all(a, axis, 0, 0, axis_index_groups=groups, tiled=True)]
    ppermute x5, waiting for transfers between devices: 16 us -> 2.62 us  [from_y(): return lax.ppermute(a, 'row', swap_y)]
    ppermute x7 -> x8, starting transfers between devices: 25.6 us -> 30.3 us  [from_core(): return lax.ppermute(a, 'row', swap_core)]
    all_to_all x4 -> x5, starting transfers between devices: 32.4 us -> 35.6 us  [exchange(): return lax.all_to_all(a, axis, 0, 0, axis_index_groups=groups, tiled=True)]
    unnamed x26 -> x22, local copies, waits for them, and re-layouts: 4.06 us -> 4.73 us
  transfers between devices with their start and end apart: 17 -> 19, of which waited for: 7 -> 7; matrix products, arithmetic and copies ran while one was open for 8% -> 7% of each run, Pallas kernels for 3% -> 4%
where the time goes in v6:
time: 146 us; the launch traced here: 145 us
  starting transfers between devices  83 us (57%)
  waiting for transfers between devices  37.8 us (26%)
  Pallas kernels  7.94 us (5%)
  local copies, waits for them, and re-layouts  7.8 us (5%)
  other arithmetic  4.68 us (3%)
  matrix products  2.75 us (2%)
    all_to_all x5, starting transfers between devices, exchange(): return lax.all_to_all(a, axis, 0, 0, axis_index_groups=groups, tiled=True)  35.6 us
    all_to_all x5, waiting for transfers between devices, exchange(): return lax.all_to_all(a, axis, 0, 0, axis_index_groups=groups, tiled=True)  30.5 us
    ppermute x8, starting transfers between devices, from_core(): return lax.ppermute(a, 'row', swap_core)  30.3 us
    ppermute x5, starting transfers between devices, from_y(): return lax.ppermute(a, 'row', swap_y)  13.5 us
    unnamed x22, local copies, waits for them, and re-layouts  4.73 us
    ppermute x1, starting transfers between devices, from_both(): return lax.ppermute(a, 'row', swap_both)  3.54 us
    ppermute x1, waiting for transfers between devices, from_both(): return lax.ppermute(a, 'row', swap_both)  3.35 us
  transfers between devices with their start and end apart: 19, of which 7 were waited for; matrix products, arithmetic and copies ran while one was open for 7% of the time, Pallas kernels for 4%

profile of v6, /device:TPU:1, one launch (start us, length us, event | category | flops | bytes accessed | tf_op | source)
XLA Modules:
  0.0 145.0 jit_solution(14183234231642990388)
XLA Ops:
  5.5 4.0 %collective-permute-start.1 = (bf16[384,768]{1,0:T(8,128)(2,1)S(1)}, bf16[384,768]{1,0:T(8,128)(2,1)S(1)}, u32[]{:S(2)}, u32[]{:S(2)}) collective-permute-start(bf16[384,768]{1,0:T(8,128)(2,1)S(1)} %get-tuple-element.14), channel_id=1, source_target_pairs={{0,256},{8,264},{16,272},{24,280},{32,288},{40,296},{48,304},{56,3... | collective-permute-start | bytes 1769480 | tf_op jit(solution)/shard_map/ppermute | solution.py:140
  9.5 6.7 %collective-permute-start = (bf16[256,768]{1,0:T(8,128)(2,1)S(1)}, bf16[256,768]{1,0:T(8,128)(2,1)S(1)}, u32[]{:S(2)}, u32[]{:S(2)}) collective-permute-start(bf16[256,768]{1,0:T(8,128)(2,1)S(1)} %get-tuple-element.15), channel_id=1, source_target_pairs={{0,8},{8,0},{16,24},{24,16},{32,40},{40,32},{48,56},{56,48},{64,72... | collective-permute-start | bytes 1179656 | tf_op jit(solution)/shard_map/ppermute | solution.py:137
  18.7 11.5 %all-to-all-start = ((bf16[32,8,768]{2,1,0:T(8,128)(2,1)}), bf16[32,8,768]{2,1,0:T(8,128)(2,1)S(1)}, u32[]{:S(2)}, u32[]{:S(2)}) async-start(bf16[32,8,768]{2,1,0:T(8,128)(2,1)} %fusion), calls=%async_computation | async-start | bytes 786432 | tf_op jit(solution)/shard_map/all_to_all | solution.py:146
  31.4 2.5 %collective-permute-start.2 = (bf16[2,384,768]{2,1,0:T(8,128)(2,1)}, bf16[2,384,768]{2,1,0:T(8,128)(2,1)}, u32[]{:S(2)}, u32[]{:S(2)}) collective-permute-start(bf16[2,384,768]{2,1,0:T(8,128)(2,1)} %pad_maximum_fusion.1), channel_id=1, source_target_pairs={{0,8},{8,0},{16,24},{24,16},{32,40},{40,32},{48,56},{56,48},{64,72... | collective-permute-start | bytes 3538952 | tf_op jit(solution)/shard_map/ppermute | solution.py:137
  35.6 3.4 %collective-permute-start.3 = (f32[2,16,384]{2,1,0:T(8,128)S(1)}, f32[2,16,384]{2,1,0:T(8,128)S(1)}, u32[]{:S(2)}, u32[]{:S(2)}) collective-permute-start(f32[2,16,384]{2,1,0:T(8,128)S(1)} %get-tuple-element.25), channel_id=1, source_target_pairs={{0,256},{8,264},{16,272},{24,280},{32,288},{40,296},{48,304},{56,3... | collective-permute-start | bytes 147464 | tf_op jit(solution)/shard_map/ppermute | solution.py:140
  39.1 2.6 %collective-permute-done.3 = f32[2,16,384]{2,1,0:T(8,128)S(1)} collective-permute-done((f32[2,16,384]{2,1,0:T(8,128)S(1)}, f32[2,16,384]{2,1,0:T(8,128)S(1)}, u32[]{:S(2)}, u32[]{:S(2)}) %collective-permute-start.3) | collective-permute-done | bytes 49184 | tf_op jit(solution)/shard_map/ppermute | solution.py:140
  41.8 2.6 %collective-permute-start.4 = (f32[2,16,384]{2,0,1:T(2,128)S(1)}, f32[2,16,384]{2,0,1:T(2,128)S(1)}, u32[]{:S(2)}, u32[]{:S(2)}) collective-permute-start(f32[2,16,384]{2,0,1:T(2,128)S(1)} %bitcast.70), channel_id=1, source_target_pairs={{0,8},{8,0},{16,24},{24,16},{32,40},{40,32},{48,56},{56,48},{64,72... | collective-permute-start | bytes 147464 | tf_op jit(solution)/shard_map/ppermute | solution.py:137
  47.0 8.9 %all-to-all-done.parts_ref = bf16[32,8,768]{2,1,0:T(8,128)(2,1)S(1)} async-done(((bf16[32,8,768]{2,1,0:T(8,128)(2,1)}), bf16[32,8,768]{2,1,0:T(8,128)(2,1)S(1)}, u32[]{:S(2)}, u32[]{:S(2)}) %all-to-all-start) | async-done | bytes 393248 | tf_op jit(solution)/shard_map/all_to_all | solution.py:146
  56.7 4.6 %all-to-all-start.1 = ((bf16[16,16,768]{2,1,0:T(8,128)(2,1)}), bf16[16,16,768]{2,1,0:T(8,128)(2,1)S(1)}, u32[]{:S(2)}, u32[]{:S(2)}) async-start(bf16[16,16,768]{2,1,0:T(8,128)(2,1)} %copy-done), calls=%async_computation.1 | async-start | bytes 786432 | tf_op jit(solution)/shard_map/all_to_all | solution.py:146
  62.7 2.1 %collective-permute-start.5 = (bf16[768,384]{1,0:T(8,128)(2,1)S(1)}, bf16[768,384]{1,0:T(8,128)(2,1)}, u32[]{:S(2)}, u32[]{:S(2)}) collective-permute-start(bf16[768,384]{1,0:T(8,128)(2,1)S(1)} %add_convert_fusion.a_ref), channel_id=1, source_target_pairs={{0,256},{8,264},{16,272},{24,280},{32,288},{40,296},{48,304},{56,3... | collective-permute-start | bytes 1769480 | tf_op jit(solution)/shard_map/ppermute | solution.py:140
  64.8 14.6 %all-to-all-done.1.got_ref = bf16[16,16,768]{2,1,0:T(8,128)(2,1)S(1)} async-done(((bf16[16,16,768]{2,1,0:T(8,128)(2,1)}), bf16[16,16,768]{2,1,0:T(8,128)(2,1)S(1)}, u32[]{:S(2)}, u32[]{:S(2)}) %all-to-all-start.1) | async-done | bytes 393248 | tf_op jit(solution)/shard_map/all_to_all | solution.py:146
  81.0 6.5 %all-to-all-start.2 = ((bf16[8,16,1536]{2,1,0:T(8,128)(2,1)}), bf16[8,16,1536]{2,1,0:T(8,128)(2,1)S(1)}, u32[]{:S(2)}, u32[]{:S(2)}) async-start(bf16[8,16,1536]{2,1,0:T(8,128)(2,1)} %bitcast.21.after_ref), calls=%async_computation.2 | async-start | bytes 786432 | tf_op jit(solution)/shard_map/all_to_all | solution.py:146
  87.6 8.6 %collective-permute-start.6 = (bf16[768,384]{1,0:T(8,128)(2,1)S(1)}, bf16[768,384]{1,0:T(8,128)(2,1)}, u32[]{:S(2)}, u32[]{:S(2)}) collective-permute-start(bf16[768,384]{1,0:T(8,128)(2,1)S(1)} %add_convert_fusion.a_ref), channel_id=1, source_target_pairs={{0,8},{8,0},{16,24},{24,16},{32,40},{40,32},{48,56},{56,48},{64,72... | collective-permute-start | bytes 1769480 | tf_op jit(solution)/shard_map/ppermute | solution.py:137
  97.3 1.9 %collective-permute-start.7 = (bf16[768,384]{1,0:T(8,128)(2,1)S(1)}, bf16[768,384]{1,0:T(8,128)(2,1)}, u32[]{:S(2)}, u32[]{:S(2)}) collective-permute-start(bf16[768,384]{1,0:T(8,128)(2,1)S(1)} %shard_map.114), channel_id=1, source_target_pairs={{0,8},{8,0},{16,24},{24,16},{32,40},{40,32},{48,56},{56,48},{64,72... | collective-permute-start | bytes 1769480 | tf_op jit(solution)/shard_map/ppermute | solution.py:137
  100.1 6.9 %all-to-all-start.3 = ((bf16[8,16,1536]{2,1,0:T(8,128)(2,1)}), bf16[8,16,1536]{2,1,0:T(8,128)(2,1)S(1)}, u32[]{:S(2)}, u32[]{:S(2)}) async-start(bf16[8,16,1536]{2,1,0:T(8,128)(2,1)} %broadcast_in_dim.23), calls=%async_computation.3 | async-start | bytes 786432 | tf_op jit(solution)/shard_map/all_to_all | solution.py:146
  107.0 2.1 %collective-permute-start.8 = (bf16[128,1536]{1,0:T(8,128)(2,1)S(1)}, bf16[128,1536]{1,0:T(8,128)(2,1)S(1)}, u32[]{:S(2)}, u32[]{:S(2)}) collective-permute-start(bf16[128,1536]{1,0:T(8,128)(2,1)S(1)} %shard_map.116.refs_0_), channel_id=1, source_target_pairs={{0,256},{8,264},{16,272},{24,280},{32,288},{40,296},{48,304},{56,3... | collective-permute-start | bytes 1179656 | tf_op jit(solution)/shard_map/ppermute | solution.py:140
  109.1 7.0 %all-to-all-done.3 = bf16[8,16,1536]{2,1,0:T(8,128)(2,1)S(1)} async-done(((bf16[8,16,1536]{2,1,0:T(8,128)(2,1)}), bf16[8,16,1536]{2,1,0:T(8,128)(2,1)S(1)}, u32[]{:S(2)}, u32[]{:S(2)}) %all-to-all-start.3) | async-done | bytes 393248 | tf_op jit(solution)/shard_map/all_to_all | solution.py:146
  116.1 2.9 %shard_map.115 = (bf16[128,768]{1,0:T(8,128)(2,1)}, bf16[128,384]{1,0:T(8,128)(2,1)S(1)}, bf16[128,384]{1,0:T(8,128)(2,1)S(1)}, bf16[128,384]{1,0:T(8,128)(2,1)S(1)}) custom-call(bf16[128,1536]{1,0:T(8,128)(2,1)S(1)} %bitcast.57, bf16[768,384]{1,0:T(8,128)(2,1)S(1)} %add_convert_fusion.a_ref, bf16[768,384]{1,0:T(8,128)(2,1)} %collective-permute-done.5.a_ref.b_ref, ...), custom_call_target="tpu_custom_call" | custom-call | flops 301989888 | bytes 3145728 | tf_op jit(solution)/shard_map/pallas_call | solution.py:242
  119.0 6.0 %all-to-all-start.4 = ((bf16[16,8,768]{2,1,0:T(8,128)(2,1)}), bf16[16,8,768]{2,1,0:T(8,128)(2,1)S(1)}, u32[]{:S(2)}, u32[]{:S(2)}) async-start(bf16[16,8,768]{2,1,0:T(8,128)(2,1)} %bitcast.23.after_ref), calls=%async_computation.4 | async-start | bytes 393216 | tf_op jit(solution)/shard_map/all_to_all | solution.py:146
  125.1 3.7 %collective-permute-start.9 = (bf16[128,1536]{1,0:T(8,128)(2,1)S(1)}, bf16[128,1536]{1,0:T(8,128)(2,1)S(1)}, u32[]{:S(2)}, u32[]{:S(2)}) collective-permute-start(bf16[128,1536]{1,0:T(8,128)(2,1)S(1)} %shard_map.116.refs_0_), channel_id=1, source_target_pairs={{0,8},{8,0},{16,24},{24,16},{32,40},{40,32},{48,56},{56,48},{64,72... | collective-permute-start | bytes 1179656 | tf_op jit(solution)/shard_map/ppermute | solution.py:137
  132.7 2.4 %collective-permute-start.12 = (bf16[128,384]{1,0:T(8,128)(2,1)S(1)}, bf16[128,384]{1,0:T(8,128)(2,1)S(1)}, u32[]{:S(2)}, u32[]{:S(2)}) collective-permute-start(bf16[128,384]{1,0:T(8,128)(2,1)S(1)} %get-tuple-element.18), channel_id=1, source_target_pairs={{0,8},{8,0},{16,24},{24,16},{32,40},{40,32},{48,56},{56,48},{64,72... | collective-permute-start | bytes 294920 | tf_op jit(solution)/shard_map/ppermute | solution.py:137
  135.1 3.5 %collective-permute-start.13 = (bf16[128,384]{1,0:T(8,128)(2,1)S(1)}, bf16[128,384]{1,0:T(8,128)(2,1)S(1)}, u32[]{:S(2)}, u32[]{:S(2)}) collective-permute-start(bf16[128,384]{1,0:T(8,128)(2,1)S(1)} %get-tuple-element.19), channel_id=1, source_target_pairs={{0,264},{8,256},{16,280},{24,272},{32,296},{40,288},{48,312},{56,3... | collective-permute-start | bytes 294920 | tf_op jit(solution)/shard_map/ppermute | solution.py:143
  138.7 3.4 %collective-permute-done.13.refs_6_ = bf16[128,384]{1,0:T(8,128)(2,1)S(1)} collective-permute-done((bf16[128,384]{1,0:T(8,128)(2,1)S(1)}, bf16[128,384]{1,0:T(8,128)(2,1)S(1)}, u32[]{:S(2)}, u32[]{:S(2)}) %collective-permute-start.13) | collective-permute-done | bytes 98336 | tf_op jit(solution)/shard_map/ppermute | solution.py:143
  142.1 2.3 %shard_map.118 = (bf16[768,384]{1,0:T(8,128)(2,1)}, bf16[384,768]{1,0:T(8,128)(2,1)}, bf16[16,128]{1,0:T(8,128)(2,1)S(1)}) custom-call(s32[2]{0:T(128)S(1)} %pad_add_fusion.at_ref, bf16[2,2,128,384]{3,2,1,0:T(8,128)(2,1)S(1)} %bitcast.61, bf16[128,1536]{1,0:T(8,128)(2,1)S(1)} %bitcast.58, bf16[128,1536]{1,0:T(8,128)(2,1)S(1)} %shard_map.116.refs_0_, ...), custom_call_target="tpu_custom_call" | custom-call | flops 603979776 | bytes 262144 | tf_op jit(solution)/shard_map/pallas_call | solution.py:264
  (71 shorter events, 23.1 us)
Async XLA Ops:
  5.5 26.0 %copy-start.1 = (bf16[2,256,384]{2,1,0:T(8,128)(2,1)}, bf16[2,256,384]{2,1,0:T(8,128)(2,1)S(1)}, u32[]{:S(2)}) copy-start(bf16[2,256,384]{2,1,0:T(8,128)(2,1)S(1)} %get-tuple-element.13) | copy-start | bytes 1179652
  5.5 24.7 %collective-permute-start.1 = (bf16[384,768]{1,0:T(8,128)(2,1)S(1)}, bf16[384,768]{1,0:T(8,128)(2,1)S(1)}, u32[]{:S(2)}, u32[]{:S(2)}) collective-permute-start(bf16[384,768]{1,0:T(8,128)(2,1)S(1)} %get-tuple-element.14), channel_id=1, source_target_pairs={{0,256},{8,264},{16,272},{24,280},{32,288},{40,296},{48,304},{56,3... | collective-permute-start | bytes 1769480 | tf_op jit(solution)/shard_map/ppermute | solution.py:140
  9.5 8.0 %collective-permute-start = (bf16[256,768]{1,0:T(8,128)(2,1)S(1)}, bf16[256,768]{1,0:T(8,128)(2,1)S(1)}, u32[]{:S(2)}, u32[]{:S(2)}) collective-permute-start(bf16[256,768]{1,0:T(8,128)(2,1)S(1)} %get-tuple-element.15), channel_id=1, source_target_pairs={{0,8},{8,0},{16,24},{24,16},{32,40},{40,32},{48,56},{56,48},{64,72... | collective-permute-start | bytes 1179656 | tf_op jit(solution)/shard_map/ppermute | solution.py:137
  18.7 20.4 %copy-start.9 = (s32[8,6]{1,0:T(8,128)S(1)}, s32[8,6]{1,0:T(8,128)}, u32[]{:S(2)}) copy-start(s32[8,6]{1,0:T(8,128)} %param.10) | copy-start | bytes 580
  18.7 25.7 %copy-start.8 = (bf16[8,768]{1,0:T(8,128)(2,1)S(1)}, bf16[8,768]{1,0:T(8,128)(2,1)}, u32[]{:S(2)}) copy-start(bf16[8,768]{1,0:T(8,128)(2,1)} %param.9) | copy-start | bytes 36868
  18.7 37.2 %all-to-all-start = ((bf16[32,8,768]{2,1,0:T(8,128)(2,1)}), bf16[32,8,768]{2,1,0:T(8,128)(2,1)S(1)}, u32[]{:S(2)}, u32[]{:S(2)}) async-start(bf16[32,8,768]{2,1,0:T(8,128)(2,1)} %fusion), calls=%async_computation | async-start | bytes 786432 | tf_op jit(solution)/shard_map/all_to_all | solution.py:146
  30.2 15.1 %copy-start.7 = (bf16[384,768]{1,0:T(8,128)(2,1)}, bf16[384,768]{1,0:T(8,128)(2,1)S(1)}, u32[]{:S(2)}) copy-start(bf16[384,768]{1,0:T(8,128)(2,1)S(1)} %collective-permute-done.1) | copy-start | bytes 1769476
  31.4 13.9 %collective-permute-start.2 = (bf16[2,384,768]{2,1,0:T(8,128)(2,1)}, bf16[2,384,768]{2,1,0:T(8,128)(2,1)}, u32[]{:S(2)}, u32[]{:S(2)}) collective-permute-start(bf16[2,384,768]{2,1,0:T(8,128)(2,1)} %pad_maximum_fusion.1), channel_id=1, source_target_pairs={{0,8},{8,0},{16,24},{24,16},{32,40},{40,32},{48,56},{56,48},{64,72... | collective-permute-start | bytes 3538952 | tf_op jit(solution)/shard_map/ppermute | solution.py:137
  35.6 6.2 %collective-permute-start.3 = (f32[2,16,384]{2,1,0:T(8,128)S(1)}, f32[2,16,384]{2,1,0:T(8,128)S(1)}, u32[]{:S(2)}, u32[]{:S(2)}) collective-permute-start(f32[2,16,384]{2,1,0:T(8,128)S(1)} %get-tuple-element.25), channel_id=1, source_target_pairs={{0,256},{8,264},{16,272},{24,280},{32,288},{40,296},{48,304},{56,3... | collective-permute-start | bytes 147464 | tf_op jit(solution)/shard_map/ppermute | solution.py:140
  41.8 3.4 %collective-permute-start.4 = (f32[2,16,384]{2,0,1:T(2,128)S(1)}, f32[2,16,384]{2,0,1:T(2,128)S(1)}, u32[]{:S(2)}, u32[]{:S(2)}) collective-permute-start(f32[2,16,384]{2,0,1:T(2,128)S(1)} %bitcast.70), channel_id=1, source_target_pairs={{0,8},{8,0},{16,24},{24,16},{32,40},{40,32},{48,56},{56,48},{64,72... | collective-permute-start | bytes 147464 | tf_op jit(solution)/shard_map/ppermute | solution.py:137
  56.7 22.7 %all-to-all-start.1 = ((bf16[16,16,768]{2,1,0:T(8,128)(2,1)}), bf16[16,16,768]{2,1,0:T(8,128)(2,1)S(1)}, u32[]{:S(2)}, u32[]{:S(2)}) async-start(bf16[16,16,768]{2,1,0:T(8,128)(2,1)} %copy-done), calls=%async_computation.1 | async-start | bytes 786432 | tf_op jit(solution)/shard_map/all_to_all | solution.py:146
  62.7 33.4 %collective-permute-start.5 = (bf16[768,384]{1,0:T(8,128)(2,1)S(1)}, bf16[768,384]{1,0:T(8,128)(2,1)}, u32[]{:S(2)}, u32[]{:S(2)}) collective-permute-start(bf16[768,384]{1,0:T(8,128)(2,1)S(1)} %add_convert_fusion.a_ref), channel_id=1, source_target_pairs={{0,256},{8,264},{16,272},{24,280},{32,288},{40,296},{48,304},{56,3... | collective-permute-start | bytes 1769480 | tf_op jit(solution)/shard_map/ppermute | solution.py:140
  81.0 18.2 %all-to-all-start.2 = ((bf16[8,16,1536]{2,1,0:T(8,128)(2,1)}), bf16[8,16,1536]{2,1,0:T(8,128)(2,1)S(1)}, u32[]{:S(2)}, u32[]{:S(2)}) async-start(bf16[8,16,1536]{2,1,0:T(8,128)(2,1)} %bitcast.21.after_ref), calls=%async_computation.2 | async-start | bytes 786432 | tf_op jit(solution)/shard_map/all_to_all | solution.py:146
  87.6 21.5 %collective-permute-start.6 = (bf16[768,384]{1,0:T(8,128)(2,1)S(1)}, bf16[768,384]{1,0:T(8,128)(2,1)}, u32[]{:S(2)}, u32[]{:S(2)}) collective-permute-start(bf16[768,384]{1,0:T(8,128)(2,1)S(1)} %add_convert_fusion.a_ref), channel_id=1, source_target_pairs={{0,8},{8,0},{16,24},{24,16},{32,40},{40,32},{48,56},{56,48},{64,72... | collective-permute-start | bytes 1769480 | tf_op jit(solution)/shard_map/ppermute | solution.py:137
  97.3 11.8 %collective-permute-start.7 = (bf16[768,384]{1,0:T(8,128)(2,1)S(1)}, bf16[768,384]{1,0:T(8,128)(2,1)}, u32[]{:S(2)}, u32[]{:S(2)}) collective-permute-start(bf16[768,384]{1,0:T(8,128)(2,1)S(1)} %shard_map.114), channel_id=1, source_target_pairs={{0,8},{8,0},{16,24},{24,16},{32,40},{40,32},{48,56},{56,48},{64,72... | collective-permute-start | bytes 1769480 | tf_op jit(solution)/shard_map/ppermute | solution.py:137
  100.1 16.1 %all-to-all-start.3 = ((bf16[8,16,1536]{2,1,0:T(8,128)(2,1)}), bf16[8,16,1536]{2,1,0:T(8,128)(2,1)S(1)}, u32[]{:S(2)}, u32[]{:S(2)}) async-start(bf16[8,16,1536]{2,1,0:T(8,128)(2,1)} %broadcast_in_dim.23), calls=%async_computation.3 | async-start | bytes 786432 | tf_op jit(solution)/shard_map/all_to_all | solution.py:146
  107.0 35.1 %copy-start.2 = (bf16[2,256,384]{2,1,0:T(8,128)(2,1)S(1)}, bf16[2,256,384]{2,1,0:T(8,128)(2,1)}, u32[]{:S(2)}) copy-start(bf16[2,256,384]{2,1,0:T(8,128)(2,1)} %copy-done.1) | copy-start | bytes 1179652
  107.0 21.8 %collective-permute-start.8 = (bf16[128,1536]{1,0:T(8,128)(2,1)S(1)}, bf16[128,1536]{1,0:T(8,128)(2,1)S(1)}, u32[]{:S(2)}, u32[]{:S(2)}) collective-permute-start(bf16[128,1536]{1,0:T(8,128)(2,1)S(1)} %shard_map.116.refs_0_), channel_id=1, source_target_pairs={{0,256},{8,264},{16,272},{24,280},{32,288},{40,296},{48,304},{56,3... | collective-permute-start | bytes 1179656 | tf_op jit(solution)/shard_map/ppermute | solution.py:140
  119.0 25.3 %all-to-all-start.4 = ((bf16[16,8,768]{2,1,0:T(8,128)(2,1)}), bf16[16,8,768]{2,1,0:T(8,128)(2,1)S(1)}, u32[]{:S(2)}, u32[]{:S(2)}) async-start(bf16[16,8,768]{2,1,0:T(8,128)(2,1)} %bitcast.23.after_ref), calls=%async_computation.4 | async-start | bytes 393216 | tf_op jit(solution)/shard_map/all_to_all | solution.py:146
  125.1 13.7 %collective-permute-start.9 = (bf16[128,1536]{1,0:T(8,128)(2,1)S(1)}, bf16[128,1536]{1,0:T(8,128)(2,1)S(1)}, u32[]{:S(2)}, u32[]{:S(2)}) collective-permute-start(bf16[128,1536]{1,0:T(8,128)(2,1)S(1)} %shard_map.116.refs_0_), channel_id=1, source_target_pairs={{0,8},{8,0},{16,24},{24,16},{32,40},{40,32},{48,56},{56,48},{64,72... | collective-permute-start | bytes 1179656 | tf_op jit(solution)/shard_map/ppermute | solution.py:137
  128.8 13.3 %collective-permute-start.10 = (bf16[128,1536]{1,0:T(8,128)(2,1)S(1)}, bf16[128,1536]{1,0:T(8,128)(2,1)S(1)}, u32[]{:S(2)}, u32[]{:S(2)}) collective-permute-start(bf16[128,1536]{1,0:T(8,128)(2,1)S(1)} %shard_map.117), channel_id=1, source_target_pairs={{0,8},{8,0},{16,24},{24,16},{32,40},{40,32},{48,56},{56,48},{64,72... | collective-permute-start | bytes 1179656 | tf_op jit(solution)/shard_map/ppermute | solution.py:137
  130.8 8.0 %collective-permute-start.11 = (bf16[128,384]{1,0:T(8,128)(2,1)S(1)}, bf16[128,384]{1,0:T(8,128)(2,1)S(1)}, u32[]{:S(2)}, u32[]{:S(2)}) collective-permute-start(bf16[128,384]{1,0:T(8,128)(2,1)S(1)} %get-tuple-element.17), channel_id=1, source_target_pairs={{0,256},{8,264},{16,272},{24,280},{32,288},{40,296},{48,304},{56,3... | collective-permute-start | bytes 294920 | tf_op jit(solution)/shard_map/ppermute | solution.py:140
  132.7 6.0 %collective-permute-start.12 = (bf16[128,384]{1,0:T(8,128)(2,1)S(1)}, bf16[128,384]{1,0:T(8,128)(2,1)S(1)}, u32[]{:S(2)}, u32[]{:S(2)}) collective-permute-start(bf16[128,384]{1,0:T(8,128)(2,1)S(1)} %get-tuple-element.18), channel_id=1, source_target_pairs={{0,8},{8,0},{16,24},{24,16},{32,40},{40,32},{48,56},{56,48},{64,72... | collective-permute-start | bytes 294920 | tf_op jit(solution)/shard_map/ppermute | solution.py:137
  135.1 7.0 %collective-permute-start.13 = (bf16[128,384]{1,0:T(8,128)(2,1)S(1)}, bf16[128,384]{1,0:T(8,128)(2,1)S(1)}, u32[]{:S(2)}, u32[]{:S(2)}) collective-permute-start(bf16[128,384]{1,0:T(8,128)(2,1)S(1)} %get-tuple-element.19), channel_id=1, source_target_pairs={{0,264},{8,256},{16,280},{24,272},{32,296},{40,288},{48,312},{56,3... | collective-permute-start | bytes 294920 | tf_op jit(solution)/shard_map/ppermute | solution.py:143
  (5 other events, 14.5 us)
